TPU v7x, 768 devices: a whole 4x8x12 slice. The times are simulated.
768 devices in a mesh: space: 192 (over z, y, core), group: 4 (over x).
Axes of the slice: x: 4, y: 8, z: 12, core: 2. Of those that a mesh axis runs over, the one named last changes fastest.
Arguments:
- snapshots: float32 [786432, 128], P(('space', 'group')), may hold values from -1500 to 1500
- last_snapshot: float32 [786432], P(('space', 'group')), may hold values from -1500 to 1500
Outputs:
- reduced_operator: float32 [128, 128], replicated
- mode_shapes: float32 [786432, 128], P(('space', 'group'))
All inputs are finite; a program needn't handle non-finite values.
Results may differ from a plain program's by a relative error of at most 0.000068.
Values sent between devices are 32-bit elements; how exact they have to be, the bound alone decides.
No kernel may reach another device: no remote copies, remote signals or barrier semaphores. Data moves between devices by JAX's collectives and lax.ppermute only.
A program may use at most 32 MiB of HBM per device.

v0:
```python
import jax
import jax.numpy as jnp
from jax import lax
from jax.sharding import PartitionSpec as P


def transpose_product(left, right):
    return lax.dot_general(
        left,
        right,
        (((0,), (0,)), ((), ())),
        precision=lax.Precision.HIGHEST,
        preferred_element_type=jnp.float32,
    )


def sum_moments(moments):
    moments = lax.psum((moments[0], moments[1]), "space")
    moments = lax.psum((moments[0], moments[1]), "group")
    return moments


def shards(snapshots, last_snapshot):
    highest = lax.Precision.HIGHEST
    second = jnp.concatenate([snapshots[:, 1:], last_snapshot[:, None]], axis=1)
    row_count = snapshots.shape[0] * lax.axis_size("space") * lax.axis_size("group")
    moment_one = transpose_product(snapshots, snapshots)
    moment_cross = transpose_product(snapshots, second)
    summed = sum_moments((moment_one, moment_cross))
    total_one = summed[0]
    total_cross = summed[1]
    factor = jnp.linalg.cholesky(total_one)
    identity = jnp.eye(total_one.shape[0], dtype=jnp.float32)
    inverse = lax.linalg.triangular_solve(factor, identity, left_side=True, lower=True).T
    middle = jnp.dot(total_cross, inverse, precision=highest, preferred_element_type=jnp.float32)
    reduced = jnp.dot(inverse.T, middle, precision=highest, preferred_element_type=jnp.float32)
    projected = jnp.dot(second, inverse, precision=highest, preferred_element_type=jnp.float32)
    column_sums = lax.psum(jnp.sum(projected * projected, axis=0), ("space", "group"))
    mean_square = column_sums / row_count
    mode_shapes = projected / jnp.sqrt(mean_square + 1e-06)[None, :]
    return (reduced, mode_shapes)


def solution(mesh):
    in_specs = (P(("space", "group"), None), P(("space", "group")))
    out_specs = (P(), P(("space", "group"), None))
    return jax.shard_map(shards, mesh=mesh, in_specs=in_specs, out_specs=out_specs, check_vma=False)
```

profile of v0, /device:TPU:1, one launch (start us, length us, event | category | flops | bytes accessed | tf_op | source)
XLA Modules:
  0.0 506.9 jit_solution(15497285613669657041)
XLA Ops:
  7.2 0.0 copy-start
  7.2 0.0 all-reduce.5.cloned.1.call-start
  7.2 3.0 fusion.7
  10.2 0.0 copy-done
  10.2 0.0 copy-start.3
  10.2 0.2 slice.13
  10.4 0.5 copy-done.3
  10.9 0.2 copy.8
  11.1 1.8 convolution_bitcast_fusion
  12.9 0.0 all-reduce.5.cloned.1.call-update
  12.9 0.0 all-reduce.7.cloned.1.call-start
  13.0 296.7 %all-reduce.5.cloned.1.call-done = (f32[128,128]{0,1:T(8,128)}, f32[128,128]{0,1:T(8,128)}) async-done(((f32[128,128]{0,1:T(8,128)}, f32[128,128]{0,1:T(8,128)}), (f32[128,128]{0,1:T(8,128)}, f32[128,128]{0,1:T(8,128)})) %all-reduce.5.cloned.1.call-update) | async-done | bytes 131088 | tf_op jit(solution)/shard_map/psum | solution.py:18
  309.7 0.0 all-reduce.7.cloned.1.call-update
  309.8 52.7 %all-reduce.7.cloned.1.call-done = (f32[128,128]{0,1:T(8,128)}, f32[128,128]{0,1:T(8,128)}) async-done(((f32[128,128]{0,1:T(8,128)}, f32[128,128]{0,1:T(8,128)}), (f32[128,128]{0,1:T(8,128)}, f32[128,128]{0,1:T(8,128)})) %all-reduce.7.cloned.1.call-update) | async-done | bytes 131088 | tf_op jit(solution)/shard_map/psum | solution.py:19
  362.5 0.0 copy-start.1
  362.5 1.0 copy.7
  363.5 0.0 copy-done.1
  363.5 11.7 %cholesky.17 = f32[128,128]{1,0:T(8,128)S(1)} custom-call(f32[128,128]{1,0:T(8,128)S(1)} %fusion.4), custom_call_target="Cholesky" | custom-call | tf_op jit(solution)/shard_map/jit(cholesky)/cholesky | solution.py:32
  375.2 0.6 compare_reduce_fusion
  375.9 0.7 fusion.1
  376.6 9.8 %custom-call.6 = f32[1,128,128]{1,2,0:T(8,128)S(1)} custom-call(f32[1,128,128]{2,1,0:T(8,128)S(1)} %fusion.1), custom_call_target="InvertDiagBlocksLowerTriangular" | custom-call | tf_op jit(solution)/shard_map/triangular_solve | solution.py:34
  386.4 0.2 fusion.2
  386.6 0.0 copy-start.2
  386.6 0.6 multiply_reduce_fusion
  387.3 110.8 %psum.39 = f32[128]{0:T(128)S(1)} all-reduce(f32[128]{0:T(128)S(1)} %get-tuple-element.6), channel_id=1, replica_groups=mesh['space'=192,'group'=4] {'space','group'}, use_global_device_ids=true, to_apply=%region_7.8 | all-reduce | flops 128 | bytes 1024 | tf_op jit(solution)/shard_map/psum | solution.py:38
  498.1 0.0 copy-done.2
  498.1 0.3 fusion.8
  498.4 0.8 fusion.9
  499.2 0.8 broadcast_divide_fusion
  (3 shorter events, 0.1 us)
Async XLA Ops:
  7.2 3.0 copy-start
  7.2 302.6 %all-reduce.5.cloned.1.call-start = ((), (), s32[]{:S(2)}) async-start(), calls=%async_computation | async-start | bytes 262144 | tf_op jit(solution)/shard_map/psum | solution.py:18
  10.2 0.7 copy-start.3
  12.9 349.5 %all-reduce.7.cloned.1.call-start = ((), (), s32[]{:S(2)}) async-start(), calls=%async_computation.1 | async-start | bytes 262144 | tf_op jit(solution)/shard_map/psum | solution.py:19
  362.5 1.0 copy-start.1
  386.6 111.5 %copy-start.2 = (f32[128,128]{0,1:T(8,128)S(1)}, f32[128,128]{0,1:T(8,128)}, u32[]{:S(2)}) copy-start(f32[128,128]{0,1:T(8,128)} %get-tuple-element.5) | copy-start | bytes 196612
Sparse Core Ops, SparseCore 0:
  13.1 296.6 all-reduce.4
  312.3 50.1 all-reduce.6
where the time goes:
time: 507 us
  waiting for transfers between devices  349 us (69%)
  blocking collectives  111 us (22%)
  other arithmetic  23.7 us (5%)
  between operations  14.1 us (3%)
  matrix products  6.8 us (1%)
    psum x1, waiting for transfers between devices, sum_moments(): moments = lax.psum((moments[0], moments[1]), 'space')  297 us
    psum x1, blocking collectives, shards(): lax.psum(jnp.sum(projected * projected, axis=0), ('space', 'group'))  111 us
    psum x1, waiting for transfers between devices, sum_moments(): moments = lax.psum((moments[0], moments[1]), 'group')  52.7 us
    another operation x3, other arithmetic, shards(): factor = jnp.linalg.cholesky(total_one)  12.4 us
    another operation x2, other arithmetic, shards(): lax.linalg.triangular_solve(factor, identity, left_side=True, lower=True)  10.5 us
  transfers between devices with their start and end apart: 2, of which 2 were waited for; matrix products, arithmetic and copies ran while one was open for 0% of the time, Pallas kernels for 0%

commit v1 on v0

v1 whole, which is shorter than its diff:
```python
import jax
import jax.numpy as jnp
from jax import lax
from jax.sharding import Mesh
from jax.sharding import PartitionSpec as P

HIGHEST = lax.Precision.HIGHEST
AXES = ("z", "y", "c", "x")
NEAR = ("y", "c")
FAR = ("z", "x")


def count(axes):
    total = 1
    for axis in axes:
        total *= lax.axis_size(axis)
    return total


def scatter_sum(table, axes):
    n = count(axes)
    blocks = table.reshape(n, table.shape[0] // n, table.shape[1])
    return lax.all_to_all(blocks, axes, 0, 0, tiled=True).sum(axis=0)


def exchange(block, axes):
    n = count(axes)
    copies = jnp.broadcast_to(block[None], (n, *block.shape))
    return lax.all_to_all(copies, axes, 0, 0, tiled=True)


def total_moments(table):
    block = scatter_sum(table, NEAR)
    block = exchange(block, FAR).sum(axis=0)
    return exchange(block, NEAR).reshape(table.shape)


def dot(left, right, dims):
    return lax.dot_general(
        left, right, (dims, ((), ())), precision=HIGHEST, preferred_element_type=jnp.float32
    )


def shards(snapshots, last_snapshot):
    k = snapshots.shape[1]
    row_count = snapshots.shape[0] * count(AXES)
    cross = dot(last_snapshot[None], snapshots, ((1,), (0,)))
    square = jnp.sum(last_snapshot * last_snapshot)
    corner = jnp.zeros((15, k), jnp.float32).at[0, 0].set(square)
    table = jnp.concatenate([dot(snapshots, snapshots, ((0,), (0,))), cross, corner])
    table = total_moments(table)
    moment_one, cross, square = table[:k], table[k], table[k + 1, 0]

    factor = jnp.linalg.cholesky(moment_one)
    identity = jnp.eye(k, dtype=jnp.float32)
    inverse = lax.linalg.triangular_solve(factor, identity, left_side=True, lower=True).T
    along = dot(inverse, cross, ((0,), (0,)))
    turned = jnp.concatenate([factor.T[:, 1:], along[:, None]], axis=1)
    reduced = dot(turned, inverse, ((1,), (0,)))
    outside = jnp.maximum(square - jnp.sum(along * along), 0.0)
    column_sums = jnp.sum(reduced * reduced, axis=0) + outside * inverse[k - 1] ** 2
    mean_square = column_sums / row_count
    second = jnp.concatenate([snapshots[:, 1:], last_snapshot[:, None]], axis=1)
    scaled = inverse / jnp.sqrt(mean_square + 1e-06)[None, :]
    return reduced, dot(second, scaled, ((1,), (0,)))


def solution(mesh):
    sizes = (12, 8, 2, 4)
    fine = Mesh(mesh.devices.reshape(sizes), AXES)
    in_specs = (P(AXES, None), P(AXES))
    out_specs = (P(), P(AXES, None))
    return jax.shard_map(shards, mesh=fine, in_specs=in_specs, out_specs=out_specs, check_vma=False)
```

time: 507 us -> 105 us (0.21)
  waiting for transfers between devices: 349 us -> 8.78 us
  blocking collectives: 111 us -> 55.8 us
  between operations: 14.1 us -> 2.03 us
    psum x2 -> x0, waiting for transfers between devices: 349 us -> none  [the longest x1 297 us: sum_moments(): moments = lax.psum((moments[0], moments[1]), 'space')]
    psum x1 -> x0, blocking collectives: 111 us -> none  [shards(): lax.psum(jnp.sum(projected * projected, axis=0), ('space', 'group'))]
    all_to_all x0 -> x2, blocking collectives: none -> 55.8 us  [the longest x1 33.6 us: exchange(): return lax.all_to_all(copies, axes, 0, 0, tiled=True)]
    all_to_all x0 -> x1, waiting for transfers between devices: none -> 8.78 us  [exchange(): return lax.all_to_all(copies, axes, 0, 0, tiled=True)]
    another operation x2 -> x1, other arithmetic: 10.5 us -> 9.81 us  [shards(): lax.linalg.triangular_solve(factor, identity, left_side=True, lower=True)]
  transfers between devices with their start and end apart: 2 -> 1, of which waited for: 2 -> 1; matrix products, arithmetic and copies ran while one was open for 0% -> 0% of each run, Pallas kernels for 0% -> 0%
where the time goes in v1:
time: 105 us; the launch traced here: 104 us
  blocking collectives  55.8 us (53%)
  other arithmetic  24.9 us (24%)
  waiting for transfers between devices  8.78 us (8%)
  matrix products  6.02 us (6%)
  starting transfers between devices  4.88 us (5%)
  between operations  2.03 us (2%)
  local copies, waits for them, and re-layouts  1.76 us (2%)
    all_to_all x1, blocking collectives, exchange(): return lax.all_to_all(copies, axes, 0, 0, tiled=True)  33.6 us
    all_to_all x1, blocking collectives, scatter_sum(): return lax.all_to_all(blocks, axes, 0, 0, tiled=True).sum(axis=0)  22.1 us
    another operation x3, other arithmetic, shards(): factor = jnp.linalg.cholesky(moment_one)  12.4 us
    another operation x1, other arithmetic, shards(): lax.linalg.triangular_solve(factor, identity, left_side=True, lower=True)  9.81 us
    all_to_all x1, waiting for transfers between devices, exchange(): return lax.all_to_all(copies, axes, 0, 0, tiled=True)  8.78 us
    dot_general x5, matrix products, dot(): lax.dot_general(left, right, (dims, ((), ())), precision=HIGHEST, preferr...  5.76 us
    all_to_all x1, starting transfers between devices, exchange(): return lax.all_to_all(copies, axes, 0, 0, tiled=True)  4.88 us
  transfers between devices with their start and end apart: 1, of which 1 were waited for; matrix products, arithmetic and copies ran while one was open for 0% of the time, Pallas kernels for 0%

profile of v1, /device:TPU:1, one launch (start us, length us, event | category | flops | bytes accessed | tf_op | source)
XLA Modules:
  0.0 104.2 jit_solution(7299815554265408317)
XLA Ops:
  0.6 1.3 %multiply_reduce_fusion.1 = f32[]{:T(128)} fusion(f32[1024]{0:T(1024)} %param.5), kind=kLoop, calls=%fused_computation.23 | loop fusion | flops 2047 | bytes 4100 | tf_op jit(solution)/shard_map/reduce_sum | solution.py:48
  1.9 0.0 copy-start
  1.9 0.0 copy-start.1
  1.9 2.3 %fusion.22 = f32[128,128]{1,0:T(8,128)S(1)} fusion(f32[1024,128]{1,0:T(8,128)} %param.4), kind=kOutput, calls=%fused_computation.37 | convolution fusion | flops 201326592 | bytes 589824 | tf_op jit(solution)/shard_map/dot_general | solution.py:39
  4.2 0.0 copy-done
  4.2 0.0 copy-done.1
  4.2 0.4 fusion.23
  4.6 0.7 select_maximum_fusion
  5.3 22.1 %all_to_all.15 = f32[16,9,128]{2,1,0:T(8,128)S(1)} all-to-all(f32[16,9,128]{2,1,0:T(8,128)S(1)} %reshape.58), channel_id=1, replica_groups=mesh['z'=12,'y'=8,'c'=2,'x'=4] {'y','c'}, dimensions={0} | all-to-all | bytes 147456 | tf_op jit(solution)/shard_map/all_to_all | solution.py:23
  27.5 33.6 %all_to_all.16 = f32[48,9,128]{2,1,0:T(8,128)S(1)} all-to-all(f32[48,9,128]{2,1,0:T(8,128)S(1)} %broadcast_in_dim.9), channel_id=1, replica_groups=mesh['z'=12,'y'=8,'c'=2,'x'=4] {'z','x'}, dimensions={0} | all-to-all | bytes 442368 | tf_op jit(solution)/shard_map/all_to_all | solution.py:29
  61.1 0.1 reduce_sum.49
  61.2 0.7 broadcast_in_dim.10
  61.9 4.9 %all-to-all-start.2 = ((f32[16,9,128]{2,1,0:T(8,128)}), f32[16,9,128]{2,1,0:T(8,128)S(1)}, u32[]{:S(2)}, u32[]{:S(2)}) async-start(f32[16,9,128]{2,1,0:T(8,128)} %broadcast_in_dim.10), calls=%async_computation.2 | async-start | bytes 262144 | tf_op jit(solution)/shard_map/all_to_all | solution.py:29
  66.7 0.2 copy.14
  67.0 0.2 slice.47
  67.2 8.8 %all-to-all-done.2 = f32[16,9,128]{2,1,0:T(8,128)S(1)} async-done(((f32[16,9,128]{2,1,0:T(8,128)}), f32[16,9,128]{2,1,0:T(8,128)S(1)}, u32[]{:S(2)}, u32[]{:S(2)}) %all-to-all-start.2) | async-done | bytes 73760 | tf_op jit(solution)/shard_map/all_to_all | solution.py:29
  76.0 0.5 slice.53
  76.5 0.1 copy.16
  76.6 11.7 %cholesky.20 = f32[128,128]{1,0:T(8,128)S(1)} custom-call(f32[128,128]{1,0:T(8,128)S(1)} %fusion.10), custom_call_target="Cholesky" | custom-call | tf_op jit(solution)/shard_map/jit(cholesky)/cholesky | solution.py:54
  88.3 0.6 compare_reduce_fusion
  89.0 0.7 fusion.12
  89.7 9.8 %custom-call.6 = f32[1,128,128]{1,2,0:T(8,128)S(1)} custom-call(f32[1,128,128]{2,1,0:T(8,128)S(1)} %get-tuple-element.15), custom_call_target="InvertDiagBlocksLowerTriangular" | custom-call | tf_op jit(solution)/shard_map/triangular_solve | solution.py:56
  99.5 0.3 fusion.8
  99.7 0.8 fusion.17
  101.8 0.9 multiply_reduce_fusion
  102.7 1.4 %fusion = f32[1024,128]{1,0:T(8,128)} fusion(f32[1024,1]{1,0:T(8,128)S(1)} %copy.14, f32[1024,127]{1,0:T(8,128)S(1)} %slice.47, f32[128]{0:T(128)S(1)} %sqrt_bitcast_fusion, f32[128,128]{0,1:T(8,128)S(1)} %fusion.8), kind=kOutput, calls=%fused_computation | convolution fusion | flops 201474048 | bytes 1114624 | tf_op jit(solution)/shard_map/dot_general | solution.py:39
  (9 shorter events, 0.1 us)
Async XLA Ops:
  1.9 2.3 %copy-start = (f32[1024,128]{1,0:T(8,128)S(1)}, f32[1024,128]{1,0:T(8,128)}, u32[]{:S(2)}) copy-start(f32[1024,128]{1,0:T(8,128)} %param.4) | copy-start | bytes 1572868
  1.9 2.3 %copy-start.1 = (f32[1024]{0:T(1024)S(1)}, f32[1024]{0:T(1024)}, u32[]{:S(2)}) copy-start(f32[1024]{0:T(1024)} %param.5) | copy-start | bytes 12292
  61.9 14.1 %all-to-all-start.2 = ((f32[16,9,128]{2,1,0:T(8,128)}), f32[16,9,128]{2,1,0:T(8,128)S(1)}, u32[]{:S(2)}, u32[]{:S(2)}) async-start(f32[16,9,128]{2,1,0:T(8,128)} %broadcast_in_dim.10), calls=%async_computation.2 | async-start | bytes 262144 | tf_op jit(solution)/shard_map/all_to_all | solution.py:29

commit v2 on v1

v2 whole, which is shorter than its diff:
```python
import functools

import jax
import jax.numpy as jnp
from jax import lax
from jax.experimental import pallas as pl
from jax.experimental.pallas import tpu as pltpu
from jax.sharding import Mesh
from jax.sharding import PartitionSpec as P

HIGHEST = lax.Precision.HIGHEST
B = 8


def dot(left, right, dims):
    return lax.dot_general(
        left, right, (dims, ((), ())), precision=HIGHEST, preferred_element_type=jnp.float32
    )


def moments_kernel(s_ref, last_ref, table_ref, turn_ref):
    rows, k = s_ref.shape
    lane = lax.broadcasted_iota(jnp.int32, (k, k), 1)
    row = lax.broadcasted_iota(jnp.int32, (k, k), 0)
    last = last_ref[...]
    columns = last.T
    total = jnp.zeros((k, k), jnp.float32)
    first = jnp.zeros((8, k), jnp.float32)
    for b in range(rows // k):
        part = s_ref[b * k : (b + 1) * k, :]
        turned = jnp.where(lane == 0, columns[:, b : b + 1], part)
        turn_ref[b * k : (b + 1) * k, :] = turned
        total += dot(part, turned, ((0,), (0,)))
        first += jnp.sum((part * part).reshape(k // 8, 8, k), axis=0)
    first = jnp.sum(first, axis=0, keepdims=True)[:, :1]
    square = jnp.sum(jnp.sum(last * last, axis=0, keepdims=True), axis=1, keepdims=True)
    total = jnp.where((row == k - 1) & (lane == 1), first, total)
    total = jnp.where((row == k - 1) & (lane == 2), square, total)
    table_ref[...] = total


def moments(s, last):
    rows, k = s.shape
    return pl.pallas_call(
        moments_kernel,
        out_shape=(
            jax.ShapeDtypeStruct((k, k), jnp.float32),
            jax.ShapeDtypeStruct((rows, k), jnp.float32),
        ),
        name="moments",
    )(s, last.reshape(rows // k, k))


def inverse_rows(w, k):
    lane = lax.broadcasted_iota(jnp.int32, (B, k), 1)
    sub = lax.broadcasted_iota(jnp.int32, (B, k), 0)
    shape = (B, k)
    out = []
    w = list(w)
    for g in range(k // B):
        at = g * B
        inside = (lane >= at) & (lane < at + B)
        raw = [jnp.broadcast_to(w[g][i : i + 1, :], shape) for i in range(B)]
        e = {}
        for i in range(B):
            for j in range(i, B):
                e[i, j] = jnp.broadcast_to(raw[i][:, at + j : at + j + 1], shape)
        p = [jnp.where(inside, (lane == at + i).astype(jnp.float32), raw[i]) for i in range(B)]
        rinv, low = [], {}
        rows = None
        for j in range(B):
            root = lax.rsqrt(e[j, j])
            r = root * root
            rinv.append(r)
            y = p[j] * root
            rows = y if rows is None else jnp.where(sub == j, y, rows)
            for i in range(j + 1, B):
                low[i, j] = e[j, i] * r
            for i in range(j + 1, B):
                for m in range(i, B):
                    e[i, m] = e[i, m] - low[i, j] * e[j, m]
                p[i] = p[i] - low[i, j] * p[j]
        out.append(rows)
        if g == k // B - 1:
            break
        q = [p[j] * rinv[j] for j in range(B)]
        for j in range(B - 1, 0, -1):
            for i in range(j):
                q[i] = q[i] - low[j, i] * q[j]
        for h in range(g + 1, k // B):
            s = [jnp.broadcast_to(w[h][:, at + j : at + j + 1], shape) for j in range(B)]
            t = [s[j] * q[j] for j in range(B)]
            while len(t) > 1:
                t = [t[n] + t[n + 1] for n in range(0, len(t), 2)]
            w[h] = jnp.where(inside, 0.0, w[h]) - t[0]
    return out


def modes_kernel(row_count, table_ref, turn_ref, reduced_ref, modes_ref):
    k = table_ref.shape[1]
    lane = lax.broadcasted_iota(jnp.int32, (k, k), 1)
    row = lax.broadcasted_iota(jnp.int32, (k, k), 0)
    table = table_ref[...]
    full = jnp.where(row <= lane, table, table.T)
    full = jnp.where((row == 0) & (lane == 0), table[k - 1 : k, 1:2], full)
    square = table[k - 1 : k, 2:3]
    cross = jnp.where(lane == 0, table, full)
    groups = inverse_rows([full[n : n + B] for n in range(0, k, B)], k)
    inv_t = jnp.where(row >= lane, jnp.concatenate(groups, axis=0), 0.0)
    turned_inv = pltpu.roll(inv_t, 1, 1)
    left = dot(inv_t, cross, ((1,), (0,)))
    reduced = dot(left, turned_inv, ((1,), (1,)))
    reduced_ref[...] = reduced
    along = jnp.sum(left * left, axis=0, keepdims=True)[:, :1]
    corner = inv_t[k - 1 : k, :]
    outside = jnp.maximum(square - along, 0.0)
    lane_row = lax.broadcasted_iota(jnp.int32, (1, k), 1)
    sums = jnp.sum(reduced * reduced, axis=0, keepdims=True)
    sums = sums + jnp.where(lane_row == k - 1, outside * corner * corner, 0.0)
    scale = lax.rsqrt(sums / row_count + 1e-06)
    modes_ref[...] = dot(turn_ref[...], turned_inv, ((1,), (1,))) * scale


def modes(row_count, table, turn):
    k = table.shape[1]
    return pl.pallas_call(
        functools.partial(modes_kernel, row_count),
        out_shape=(
            jax.ShapeDtypeStruct((k, k), jnp.float32),
            jax.ShapeDtypeStruct(turn.shape, jnp.float32),
        ),
        name="modes",
    )(table, turn)


AXES = ("z", "y", "c", "x")
NEAR = ("y", "c")
FAR = ("z", "x")


def count(axes):
    total = 1
    for axis in axes:
        total *= lax.axis_size(axis)
    return total


def scatter_sum(table, axes):
    n = count(axes)
    blocks = table.reshape(n, table.shape[0] // n, table.shape[1])
    return lax.all_to_all(blocks, axes, 0, 0, tiled=True).sum(axis=0)


def exchange(block, axes):
    n = count(axes)
    copies = jnp.broadcast_to(block[None], (n, *block.shape))
    return lax.all_to_all(copies, axes, 0, 0, tiled=True)


def total_moments(table):
    block = scatter_sum(table, NEAR)
    block = exchange(block, FAR).sum(axis=0)
    return exchange(block, NEAR).reshape(table.shape)


def shards(snapshots, last_snapshot):
    row_count = snapshots.shape[0] * count(AXES)
    table, turn = moments(snapshots, last_snapshot)
    return modes(row_count, total_moments(table), turn)


def solution(mesh):
    sizes = (12, 8, 2, 4)
    fine = Mesh(mesh.devices.reshape(sizes), AXES)
    in_specs = (P(AXES, None), P(AXES))
    out_specs = (P(), P(AXES, None))
    return jax.shard_map(shards, mesh=fine, in_specs=in_specs, out_specs=out_specs, check_vma=False)
```

time: 105 us -> 74.2 us (0.71)
  other arithmetic: 24.9 us -> 0.07 us
  Pallas kernels: 0 us -> 11.3 us
  waiting for transfers between devices: 8.78 us -> 0 us
  blocking collectives: 55.8 us -> 61.9 us
  matrix products: 6.02 us -> 0 us
  starting transfers between devices: 4.88 us -> 0 us
  local copies, waits for them, and re-layouts: 1.76 us -> 0.03 us
  between operations: 2.03 us -> 0.64 us
    another operation x4 -> x0, other arithmetic: 22.2 us -> none  [the longest x3 12.4 us: shards(): factor = jnp.linalg.cholesky(moment_one)]
    pallas_call x0 -> x2, Pallas kernels: none -> 11.3 us  [the longest x1 8.75 us: modes(): pl.pallas_call(functools.partial(modes_kernel, row_count), out_shape=(jax...]
    all_to_all x1 -> x0, waiting for transfers between devices: 8.78 us -> none  [exchange(): return lax.all_to_all(copies, axes, 0, 0, tiled=True)]
    all_to_all x1 -> x2, blocking collectives: 33.6 us -> 40.3 us  [exchange(): return lax.all_to_all(copies, axes, 0, 0, tiled=True)]
    dot_general x5 -> x0, matrix products: 5.76 us -> none  [dot(): lax.dot_general(left, right, (dims, ((), ())), precision=HIGHEST, preferr...]
    all_to_all x1 -> x0, starting transfers between devices: 4.88 us -> none  [exchange(): return lax.all_to_all(copies, axes, 0, 0, tiled=True)]
    reduce_sum x1 -> x0, other arithmetic: 1.29 us -> none  [shards(): square = jnp.sum(last_snapshot * last_snapshot)]
  transfers between devices with their start and end apart: 1 -> 0, of which waited for: 1 -> 0; matrix products, arithmetic and copies ran while one was open for 0% -> 0% of each run, Pallas kernels for 0% -> 0%
where the time goes in v2:
time: 74.2 us; the launch traced here: 74 us
  blocking collectives  61.9 us (83%)
  Pallas kernels  11.3 us (15%)
    all_to_all x2, blocking collectives, exchange(): return lax.all_to_all(copies, axes, 0, 0, tiled=True)  40.3 us
    all_to_all x1, blocking collectives, scatter_sum(): return lax.all_to_all(blocks, axes, 0, 0, tiled=True).sum(axis=0)  21.6 us
    pallas_call x1, Pallas kernels, modes(): pl.pallas_call(functools.partial(modes_kernel, row_count), out_shape=(jax...  8.75 us
    pallas_call x1, Pallas kernels, moments(): pl.pallas_call(moments_kernel, out_shape=(jax.ShapeDtypeStruct((k, k), jn...  2.53 us

profile of v2, /device:TPU:1, one launch (start us, length us, event | category | flops | bytes accessed | tf_op | source)
XLA Modules:
  0.0 74.0 jit_solution(9313197829050942944)
XLA Ops:
  0.6 2.5 %moments.1 = (f32[128,128]{1,0:T(8,128)}, f32[1024,128]{1,0:T(8,128)}) custom-call(f32[1024,128]{1,0:T(8,128)} %s_ref.1, f32[8,128]{1,0:T(8,128)} %bitcast.5), custom_call_target="tpu_custom_call" | custom-call | tf_op jit(solution)/shard_map/moments/pallas_call | solution.py:44
  3.2 21.6 %all_to_all.15 = f32[16,8,128]{2,1,0:T(8,128)S(1)} all-to-all(f32[16,8,128]{2,1,0:T(8,128)} %bitcast.4), channel_id=1, replica_groups=mesh['z'=12,'y'=8,'c'=2,'x'=4] {'y','c'}, dimensions={0} | all-to-all | bytes 131072 | tf_op jit(solution)/shard_map/all_to_all | solution.py:151
  24.8 27.3 %all_to_all.16 = f32[48,8,128]{2,1,0:T(8,128)S(1)} all-to-all(f32[48,8,128]{2,1,0:T(8,128)S(1)} %broadcast_in_dim.4), channel_id=1, replica_groups=mesh['z'=12,'y'=8,'c'=2,'x'=4] {'z','x'}, dimensions={0} | all-to-all | bytes 393216 | tf_op jit(solution)/shard_map/all_to_all | solution.py:157
  52.1 0.1 reduce_sum.19
  52.2 13.0 %all_to_all.17 = f32[16,8,128]{2,1,0:T(8,128)} all-to-all(f32[16,8,128]{2,1,0:T(8,128)S(1)} %broadcast_in_dim.5), channel_id=1, replica_groups=mesh['z'=12,'y'=8,'c'=2,'x'=4] {'y','c'}, dimensions={0} | all-to-all | bytes 131072 | tf_op jit(solution)/shard_map/all_to_all | solution.py:157
  65.2 8.7 %modes.1 = (f32[128,128]{1,0:T(8,128)}, f32[1024,128]{1,0:T(8,128)}) custom-call(f32[128,128]{1,0:T(8,128)} %bitcast.3, f32[1024,128]{1,0:T(8,128)} %get-tuple-element.5.turn_ref), custom_call_target="tpu_custom_call" | custom-call | tf_op jit(solution)/shard_map/modes/pallas_call | solution.py:126
  (3 shorter events, 0.0 us)

commit v3 on v2

v3 whole, which is shorter than its diff:
```python
import functools

import jax
import jax.numpy as jnp
from jax import lax
from jax.experimental import pallas as pl
from jax.experimental.pallas import tpu as pltpu
from jax.sharding import Mesh
from jax.sharding import PartitionSpec as P

HIGHEST = lax.Precision.HIGHEST
B = 8
VMEM_BYTES = 16 * 2**20


def dot(left, right, dims):
    return lax.dot_general(
        left, right, (dims, ((), ())), precision=HIGHEST, preferred_element_type=jnp.float32
    )


def split(x):
    high = x.astype(jnp.bfloat16)
    rest = x - high.astype(jnp.float32)
    middle = rest.astype(jnp.bfloat16)
    return high, middle, (rest - middle.astype(jnp.float32)).astype(jnp.bfloat16)


def product(left, right):
    return lax.dot_general(
        left, right, (((1,), (0,)), ((), ())), preferred_element_type=jnp.float32
    )


def gram(s, last):
    rows, k = s.shape
    sub = lax.broadcasted_iota(jnp.int32, (16, k), 0)
    spread = jnp.concatenate([last, jnp.zeros_like(last)], axis=0)
    spread = jnp.concatenate([jnp.where(sub == b, spread, 0.0) for b in range(rows // k)], axis=1)
    high, middle, low = split(s)
    last_high, last_middle, last_low = split(spread)
    lead = jnp.concatenate([high.T, last_high], axis=0)
    first = product(lead, jnp.concatenate([high, middle], axis=1))
    second = product(lead, low)
    third = product(jnp.concatenate([middle.T, last_middle], axis=0), middle)
    fourth = product(jnp.concatenate([last_middle, last_low], axis=0), high)
    mixed = first[:k, k:] + second[:k]
    square = (mixed + mixed.T) + third[:k] + first[:k, :k]
    cross = fourth[16:] + second[k:] + third[k:] + first[k:, k:] + fourth[:16] + first[k:, :k]
    return square, jnp.sum(cross, axis=0, keepdims=True)


def moments_kernel(s_ref, last_ref, table_ref):
    k = s_ref.shape[1]
    last = last_ref[...]
    square, along = gram(s_ref[...], last)
    norm = jnp.sum(jnp.sum(last * last, axis=0, keepdims=True), axis=1, keepdims=True)
    sub = lax.broadcasted_iota(jnp.int32, (8, k), 0)
    lane = lax.broadcasted_iota(jnp.int32, (8, k), 1)
    tail = jnp.where((sub == 7) & (lane < k - 1), along, square[k - 8 :])
    tail = jnp.where((sub == 6) & (lane == 0), along[:, k - 1 :], tail)
    table_ref[0 : k - 8, :] = square[: k - 8]
    table_ref[k - 8 :, :] = jnp.where((sub == 6) & (lane == 1), norm, tail)


def moments(s, last):
    rows, k = s.shape
    return pl.pallas_call(
        moments_kernel,
        out_shape=jax.ShapeDtypeStruct((k, k), jnp.float32),
        name="moments",
    )(s, last.reshape(rows // k, k))


def turn_kernel(s_ref, last_ref, turn_ref):
    rows, k = s_ref.shape
    lane = lax.broadcasted_iota(jnp.int32, (k, k), 1)
    columns = last_ref[...].T
    for b in range(rows // k):
        part = s_ref[b * k : (b + 1) * k, :]
        turn_ref[b * k : (b + 1) * k, :] = jnp.where(lane == 0, columns[:, b : b + 1], part)


def turn_columns(s, last):
    rows, k = s.shape
    return pl.pallas_call(
        turn_kernel,
        out_shape=jax.ShapeDtypeStruct((rows, k), jnp.float32),
        compiler_params=pltpu.CompilerParams(vmem_limit_bytes=VMEM_BYTES),
        cost_estimate=pl.CostEstimate(flops=rows * k, bytes_accessed=8 * rows * k, transcendentals=0),
        name="turn_columns",
    )(s, last.reshape(rows // k, k))


def inverse_rows(w, k):
    lane = lax.broadcasted_iota(jnp.int32, (B, k), 1)
    sub = lax.broadcasted_iota(jnp.int32, (B, k), 0)

    def wide(column):
        return jnp.broadcast_to(column, (B, k))

    out, w = [], list(w)
    groups = k // B
    for g in range(groups):
        at = g * B
        inside = (lane >= at) & (lane < at + B)
        columns = [wide(w[g][:, at + j : at + j + 1]) for j in range(B)]
        e = {(i, j): wide(columns[j][i : i + 1, :]) for j in range(B) for i in range(j + 1)}
        p = [
            jnp.where(inside, (lane == at + i).astype(jnp.float32), wide(w[g][i : i + 1, :]))
            for i in range(B)
        ]
        inner = g < groups - 1
        if inner:
            s = [wide(w[g + 1][:, at + j : at + j + 1]) for j in range(B)]
            after = jnp.where(inside, 0.0, w[g + 1])
        low, inv, pivot = {}, [None] * B, [None] * B
        for j in range(0, B, 2):
            n = j + 1
            a, b, c = e[j, j], e[j, n], e[n, n]
            ra, rd = 1.0 / a, 1.0 / (a * c - b * b)
            rs = a * rd
            inv[j], inv[n] = ra, rs
            for i in range(n, B):
                low[i, j] = e[j, i] * ra
            for m in range(j + 2, B):
                e[n, m] = e[n, m] - low[n, j] * e[j, m]
                low[m, n] = e[n, m] * rs
            pivot[j], pivot[n] = a, c - low[n, j] * b
            p[n] = p[n] - low[n, j] * p[j]
            for i in range(j + 2, B):
                for m in range(i, B):
                    e[i, m] = (e[i, m] - low[i, j] * e[j, m]) - low[i, n] * e[n, m]
                p[i] = (p[i] - low[i, j] * p[j]) - low[i, n] * p[n]
            if inner:
                s[n] = s[n] - s[j] * low[n, j]
                for m in range(j + 2, B):
                    s[m] = (s[m] - s[j] * low[m, j]) - s[n] * low[m, n]
                after = after - (s[j] * (p[j] * ra) + s[n] * (p[n] * rs))
        rows = None
        for j in range(B):
            y = p[j] * lax.rsqrt(pivot[j])
            rows = y if rows is None else jnp.where(sub == j, y, rows)
        out.append(rows)
        if not inner:
            break
        w[g + 1] = after
        if g + 2 == groups:
            continue
        q = [p[j] * inv[j] for j in range(B)]
        for j in range(B - 1, 0, -1):
            for i in range(j):
                q[i] = q[i] - low[j, i] * q[j]
        for h in range(g + 2, groups):
            t = [wide(w[h][:, at + j : at + j + 1]) * q[j] for j in range(B)]
            while len(t) > 1:
                t = [t[n] + t[n + 1] for n in range(0, len(t), 2)]
            w[h] = jnp.where(inside, 0.0, w[h]) - t[0]
    return out


def modes_kernel(row_count, chunks, table_ref, turn_ref, reduced_hbm, modes_hbm, full_modes, small, sems):
    k = table_ref.shape[1]
    lane = lax.broadcasted_iota(jnp.int32, (k, k), 1)
    row = lax.broadcasted_iota(jnp.int32, (k, k), 0)
    table = table_ref[...]
    flip = table.T
    full = jnp.where(row <= lane, table, flip)
    last = jnp.where(row == k - 1, table[k - 2 : k - 1, 0:1], flip[:, k - 1 : k])
    square = table[k - 2 : k - 1, 1:2]
    cross = jnp.where(lane == 0, last, full)
    diagonal = jnp.where(row == lane, full, 0.0)
    across = lax.rsqrt(jnp.sum(diagonal, axis=0, keepdims=True))
    down = lax.rsqrt(jnp.sum(diagonal, axis=1, keepdims=True))
    unit = full * across * down
    groups = inverse_rows([unit[n : n + B] for n in range(0, k, B)], k)
    inv_t = jnp.where(row >= lane, jnp.concatenate(groups, axis=0), 0.0) * across
    turned_inv = pltpu.roll(inv_t, 1, 1)
    left = dot(inv_t, cross, ((1,), (0,)))
    full_modes[...] = dot(turn_ref[...], turned_inv, ((1,), (1,)))
    reduced = dot(left, turned_inv, ((1,), (1,)))
    small[...] = reduced
    copies = [pltpu.make_async_copy(small, reduced_hbm, sems.at[chunks])]
    copies[0].start()
    along = jnp.sum(left * left, axis=0, keepdims=True)[:, :1]
    corner = inv_t[k - 1 : k, :]
    outside = jnp.maximum(square - along, 0.0)
    lane_row = lax.broadcasted_iota(jnp.int32, (1, k), 1)
    sums = jnp.sum(reduced * reduced, axis=0, keepdims=True)
    sums = sums + jnp.where(lane_row == k - 1, outside * corner * corner, 0.0)
    scale = lax.rsqrt(sums / row_count + 1e-06)
    size = full_modes.shape[0] // chunks
    for n in range(chunks):
        part = pl.ds(n * size, size)
        full_modes[part, :] = full_modes[part, :] * scale
        copies.append(pltpu.make_async_copy(full_modes.at[part, :], modes_hbm.at[part, :], sems.at[n]))
        copies[-1].start()
    for copy in copies:
        copy.wait()


def modes(row_count, table, turn, chunks=4):
    k = table.shape[1]
    return pl.pallas_call(
        functools.partial(modes_kernel, row_count, chunks),
        out_shape=(
            jax.ShapeDtypeStruct((k, k), jnp.float32),
            jax.ShapeDtypeStruct(turn.shape, jnp.float32),
        ),
        in_specs=[pl.BlockSpec(memory_space=pltpu.VMEM)] * 2,
        out_specs=(pl.BlockSpec(memory_space=pl.ANY),) * 2,
        scratch_shapes=[
            pltpu.VMEM(turn.shape, jnp.float32),
            pltpu.VMEM((k, k), jnp.float32),
            pltpu.SemaphoreType.DMA((chunks + 1,)),
        ],
        compiler_params=pltpu.CompilerParams(vmem_limit_bytes=VMEM_BYTES),
        name="modes",
    )(table, turn)


AXES = ("z", "y", "c", "x")
NEAR = ("y", "c")
FAR = ("z", "x")


def count(axes):
    total = 1
    for axis in axes:
        total *= lax.axis_size(axis)
    return total


def scatter_sum(table, axes):
    n = count(axes)
    blocks = table.reshape(n, table.shape[0] // n, table.shape[1])
    return lax.all_to_all(blocks, axes, 0, 0, tiled=True).sum(axis=0)


def exchange(block, axes):
    n = count(axes)
    copies = jnp.broadcast_to(block[None], (n, *block.shape))
    return lax.all_to_all(copies, axes, 0, 0, tiled=True)


def total_moments(table):
    block = scatter_sum(table, NEAR)
    block = exchange(block, FAR).sum(axis=0)
    return exchange(block, NEAR).reshape(table.shape)


def shards(snapshots, last_snapshot):
    row_count = snapshots.shape[0] * count(AXES)
    table = moments(snapshots, last_snapshot)
    turn = turn_columns(snapshots, last_snapshot)
    return modes(row_count, total_moments(table), turn)


def solution(mesh):
    sizes = (12, 8, 2, 4)
    fine = Mesh(mesh.devices.reshape(sizes), AXES)
    in_specs = (P(AXES, None), P(AXES))
    out_specs = (P(), P(AXES, None))
    return jax.shard_map(shards, mesh=fine, in_specs=in_specs, out_specs=out_specs, check_vma=False)
```

time: 74.2 us -> 72 us (0.970)
  blocking collectives: 61.9 us -> 49 us
  waiting for transfers between devices: 0 us -> 7.5 us
  starting transfers between devices: 0 us -> 5.55 us
  Pallas kernels: 11.3 us -> 8.2 us
    all_to_all x2 -> x1, blocking collectives: 40.3 us -> 27.4 us  [exchange(): return lax.all_to_all(copies, axes, 0, 0, tiled=True)]
    all_to_all x0 -> x1, waiting for transfers between devices: none -> 7.5 us  [exchange(): return lax.all_to_all(copies, axes, 0, 0, tiled=True)]
    all_to_all x0 -> x1, starting transfers between devices: none -> 5.55 us  [exchange(): return lax.all_to_all(copies, axes, 0, 0, tiled=True)]
    pallas_call x2 -> x3, Pallas kernels: 11.3 us -> 8.2 us  [the longest x1 5.65 us: modes(): pl.pallas_call(functools.partial(modes_kernel, row_count, chunks), out_sh...]
  transfers between devices with their start and end apart: 0 -> 1, of which waited for: 0 -> 1; matrix products, arithmetic and copies ran while one was open for 0% -> 0% of each run, Pallas kernels for 0% -> 0%
where the time goes in v3:
time: 72 us; the launch traced here: 71.7 us
  blocking collectives  49 us (68%)
  Pallas kernels  8.2 us (11%)
  waiting for transfers between devices  7.5 us (10%)
  starting transfers between devices  5.55 us (8%)
    all_to_all x1, blocking collectives, exchange(): return lax.all_to_all(copies, axes, 0, 0, tiled=True)  27.4 us
    all_to_all x1, blocking collectives, scatter_sum(): return lax.all_to_all(blocks, axes, 0, 0, tiled=True).sum(axis=0)  21.6 us
    all_to_all x1, waiting for transfers between devices, exchange(): return lax.all_to_all(copies, axes, 0, 0, tiled=True)  7.5 us
    pallas_call x1, Pallas kernels, modes(): pl.pallas_call(functools.partial(modes_kernel, row_count, chunks), out_sh...  5.65 us
    all_to_all x1, starting transfers between devices, exchange(): return lax.all_to_all(copies, axes, 0, 0, tiled=True)  5.55 us
    pallas_call x1, Pallas kernels, moments(): pl.pallas_call(moments_kernel, out_shape=jax.ShapeDtypeStruct((k, k), jnp...  2.23 us
  transfers between devices with their start and end apart: 1, of which 1 were waited for; matrix products, arithmetic and copies ran while one was open for 0% of the time, Pallas kernels for 0%

profile of v3, /device:TPU:1, one launch (start us, length us, event | category | flops | bytes accessed | tf_op | source)
XLA Modules:
  0.0 71.7 jit_solution(31651635252119350)
XLA Ops:
  0.6 2.2 %moments.1 = f32[128,128]{1,0:T(8,128)} custom-call(f32[1024,128]{1,0:T(8,128)} %s_ref.3, f32[8,128]{1,0:T(8,128)} %bitcast.4), custom_call_target="tpu_custom_call" | custom-call | tf_op jit(solution)/shard_map/moments/pallas_call | solution.py:68
  2.9 21.6 %all_to_all.15 = f32[16,8,128]{2,1,0:T(8,128)S(1)} all-to-all(f32[16,8,128]{2,1,0:T(8,128)} %bitcast.6), channel_id=1, replica_groups=mesh['z'=12,'y'=8,'c'=2,'x'=4] {'y','c'}, dimensions={0} | all-to-all | bytes 131072 | tf_op jit(solution)/shard_map/all_to_all | solution.py:237
  24.5 0.0 copy-start
  24.5 27.4 %all_to_all.16 = f32[48,8,128]{2,1,0:T(8,128)S(1)} all-to-all(f32[48,8,128]{2,1,0:T(8,128)S(1)} %broadcast_in_dim.4), channel_id=1, replica_groups=mesh['z'=12,'y'=8,'c'=2,'x'=4] {'z','x'}, dimensions={0} | all-to-all | bytes 393216 | tf_op jit(solution)/shard_map/all_to_all | solution.py:243
  51.9 0.1 reduce_sum.19
  52.0 0.6 broadcast_in_dim.5
  52.6 0.0 copy-start.1
  52.6 5.5 %all-to-all-start.2 = ((f32[16,8,128]{2,1,0:T(8,128)}), f32[16,8,128]{2,1,0:T(8,128)S(1)}, u32[]{:S(2)}, u32[]{:S(2)}) async-start(f32[16,8,128]{2,1,0:T(8,128)} %broadcast_in_dim.5), calls=%async_computation.2 | async-start | bytes 131072 | tf_op jit(solution)/shard_map/all_to_all | solution.py:243
  58.2 0.0 copy-done
  58.2 0.0 copy-done.1
  58.2 0.3 turn_columns.1.turn_ref
  58.5 7.5 %all-to-all-done.2 = f32[16,8,128]{2,1,0:T(8,128)S(1)} async-done(((f32[16,8,128]{2,1,0:T(8,128)}), f32[16,8,128]{2,1,0:T(8,128)S(1)}, u32[]{:S(2)}, u32[]{:S(2)}) %all-to-all-start.2) | async-done | bytes 65568 | tf_op jit(solution)/shard_map/all_to_all | solution.py:243
  66.0 5.6 %modes.1 = (f32[128,128]{1,0:T(8,128)}, f32[1024,128]{1,0:T(8,128)}) custom-call(f32[128,128]{1,0:T(8,128)S(1)} %bitcast.3, f32[1024,128]{1,0:T(8,128)S(1)} %turn_columns.1.turn_ref), custom_call_target="tpu_custom_call" | custom-call | tf_op jit(solution)/shard_map/modes/pallas_call | solution.py:204
  (2 shorter events, 0.0 us)
Async XLA Ops:
  24.5 33.7 %copy-start = (f32[1024,128]{1,0:T(8,128)S(1)}, f32[1024,128]{1,0:T(8,128)}, u32[]{:S(2)}) copy-start(f32[1024,128]{1,0:T(8,128)} %s_ref.3) | copy-start | bytes 1572868
  52.6 5.6 %copy-start.1 = (f32[1024]{0:T(1024)S(1)}, f32[1024]{0:T(1024)}, u32[]{:S(2)}) copy-start(f32[1024]{0:T(1024)} %param.3) | copy-start | bytes 12292
  52.6 13.4 %all-to-all-start.2 = ((f32[16,8,128]{2,1,0:T(8,128)}), f32[16,8,128]{2,1,0:T(8,128)S(1)}, u32[]{:S(2)}, u32[]{:S(2)}) async-start(f32[16,8,128]{2,1,0:T(8,128)} %broadcast_in_dim.5), calls=%async_computation.2 | async-start | bytes 131072 | tf_op jit(solution)/shard_map/all_to_all | solution.py:243

commit v4 on v3

--- a/solution.py
+++ b/solution.py
@@ -10,7 +10,8 @@
 
 HIGHEST = lax.Precision.HIGHEST
 B = 8
-VMEM_BYTES = 16 * 2**20
+VMEM_BYTES = 62000000
+TURN_AT = 8
 
 
 def dot(left, right, dims):
@@ -52,47 +53,31 @@
 
 def moments_kernel(s_ref, last_ref, table_ref):
     k = s_ref.shape[1]
+    h = k // 2
     last = last_ref[...]
     square, along = gram(s_ref[...], last)
     norm = jnp.sum(jnp.sum(last * last, axis=0, keepdims=True), axis=1, keepdims=True)
-    sub = lax.broadcasted_iota(jnp.int32, (8, k), 0)
-    lane = lax.broadcasted_iota(jnp.int32, (8, k), 1)
-    tail = jnp.where((sub == 7) & (lane < k - 1), along, square[k - 8 :])
-    tail = jnp.where((sub == 6) & (lane == 0), along[:, k - 1 :], tail)
-    table_ref[0 : k - 8, :] = square[: k - 8]
-    table_ref[k - 8 :, :] = jnp.where((sub == 6) & (lane == 1), norm, tail)
-
-
-def moments(s, last):
+    row = lax.broadcasted_iota(jnp.int32, (h, k), 0)
+    lane = lax.broadcasted_iota(jnp.int32, (h, k), 1)
+    end = square[h:]
+    table_ref[0:h, :] = jnp.where((lane < h) & (row > lane), pltpu.roll(end, h, 1), square[:h])
+    diagonal = jnp.sum(jnp.where(row + h == lane, end, 0.0), axis=0, keepdims=True)
+    diagonal = jnp.where(lane[:1] == 0, norm, diagonal)
+    rest = table_ref.shape[0] - h
+    sub = lax.broadcasted_iota(jnp.int32, (rest, k), 0)
+    table_ref[h:, :] = jnp.where(sub == 0, along, jnp.where(sub == 1, diagonal, 0.0))
+
+
+def moments(s, last, table_rows):
     rows, k = s.shape
     return pl.pallas_call(
         moments_kernel,
-        out_shape=jax.ShapeDtypeStruct((k, k), jnp.float32),
+        out_shape=jax.ShapeDtypeStruct((table_rows, k), jnp.float32),
         name="moments",
     )(s, last.reshape(rows // k, k))
 
 
-def turn_kernel(s_ref, last_ref, turn_ref):
-    rows, k = s_ref.shape
-    lane = lax.broadcasted_iota(jnp.int32, (k, k), 1)
-    columns = last_ref[...].T
-    for b in range(rows // k):
-        part = s_ref[b * k : (b + 1) * k, :]
-        turn_ref[b * k : (b + 1) * k, :] = jnp.where(lane == 0, columns[:, b : b + 1], part)
-
-
-def turn_columns(s, last):
-    rows, k = s.shape
-    return pl.pallas_call(
-        turn_kernel,
-        out_shape=jax.ShapeDtypeStruct((rows, k), jnp.float32),
-        compiler_params=pltpu.CompilerParams(vmem_limit_bytes=VMEM_BYTES),
-        cost_estimate=pl.CostEstimate(flops=rows * k, bytes_accessed=8 * rows * k, transcendentals=0),
-        name="turn_columns",
-    )(s, last.reshape(rows // k, k))
-
-
-def inverse_rows(w, k):
+def inverse_rows(w, k, between):
     lane = lax.broadcasted_iota(jnp.int32, (B, k), 1)
     sub = lax.broadcasted_iota(jnp.int32, (B, k), 0)
 
@@ -102,6 +87,8 @@
     out, w = [], list(w)
     groups = k // B
     for g in range(groups):
+        if g in between:
+            between[g]()
         at = g * B
         inside = (lane >= at) & (lane < at + B)
         columns = [wide(w[g][:, at + j : at + j + 1]) for j in range(B)]
@@ -159,21 +146,47 @@
     return out
 
 
-def modes_kernel(row_count, chunks, table_ref, turn_ref, reduced_hbm, modes_hbm, full_modes, small, sems):
+def unfold(table):
+    k = table.shape[1]
+    h = k // 2
+    row = lax.broadcasted_iota(jnp.int32, (h, k), 0)
+    lane = lax.broadcasted_iota(jnp.int32, (h, k), 1)
+    flip = jnp.concatenate([table, jnp.zeros((k - table.shape[0], k), jnp.float32)], axis=0).T
+    head = table[:h]
+    top = jnp.where((lane >= h) | (row <= lane), head, flip[:h])
+    end = pltpu.roll(jnp.where(row > lane, head, flip[:h]), h, 1)
+    end = jnp.where(row + h == lane, table[h + 1 : h + 2, :], end)
+    bottom = jnp.where(lane < h, flip[h:], end)
+    return jnp.concatenate([top, bottom], axis=0), flip[:, h : h + 1], table[h + 1 : h + 2, 0:1]
+
+
+def modes_kernel(row_count, chunks, table_ref, s_hbm, last_hbm, reduced_hbm, modes_hbm, *scratch):
+    turn_ref, last_ref, full_modes, small, sems, in_sems = scratch
     k = table_ref.shape[1]
+    loads = [
+        pltpu.make_async_copy(last_hbm, last_ref, in_sems.at[0]),
+        pltpu.make_async_copy(s_hbm, turn_ref, in_sems.at[1]),
+    ]
+    for load in loads:
+        load.start()
     lane = lax.broadcasted_iota(jnp.int32, (k, k), 1)
     row = lax.broadcasted_iota(jnp.int32, (k, k), 0)
-    table = table_ref[...]
-    flip = table.T
-    full = jnp.where(row <= lane, table, flip)
-    last = jnp.where(row == k - 1, table[k - 2 : k - 1, 0:1], flip[:, k - 1 : k])
-    square = table[k - 2 : k - 1, 1:2]
+    full, last, square = unfold(table_ref[...])
     cross = jnp.where(lane == 0, last, full)
     diagonal = jnp.where(row == lane, full, 0.0)
     across = lax.rsqrt(jnp.sum(diagonal, axis=0, keepdims=True))
     down = lax.rsqrt(jnp.sum(diagonal, axis=1, keepdims=True))
     unit = full * across * down
-    groups = inverse_rows([unit[n : n + B] for n in range(0, k, B)], k)
+
+    def turn_columns():
+        for load in loads:
+            load.wait()
+        columns = last_ref[...].T
+        for b in range(turn_ref.shape[0] // k):
+            part = slice(b * k, (b + 1) * k)
+            turn_ref[part, :] = jnp.where(lane == 0, columns[:, b : b + 1], turn_ref[part, :])
+
+    groups = inverse_rows([unit[n : n + B] for n in range(0, k, B)], k, {TURN_AT: turn_columns})
     inv_t = jnp.where(row >= lane, jnp.concatenate(groups, axis=0), 0.0) * across
     turned_inv = pltpu.roll(inv_t, 1, 1)
     left = dot(inv_t, cross, ((1,), (0,)))
@@ -199,29 +212,37 @@
         copy.wait()
 
 
-def modes(row_count, table, turn, chunks=4):
-    k = table.shape[1]
+def modes(row_count, table, s, last, chunks=4):
+    rows, k = s.shape
     return pl.pallas_call(
         functools.partial(modes_kernel, row_count, chunks),
         out_shape=(
             jax.ShapeDtypeStruct((k, k), jnp.float32),
-            jax.ShapeDtypeStruct(turn.shape, jnp.float32),
+            jax.ShapeDtypeStruct(s.shape, jnp.float32),
         ),
-        in_specs=[pl.BlockSpec(memory_space=pltpu.VMEM)] * 2,
+        in_specs=[
+            pl.BlockSpec(memory_space=pltpu.VMEM),
+            pl.BlockSpec(memory_space=pl.ANY),
+            pl.BlockSpec(memory_space=pl.ANY),
+        ],
         out_specs=(pl.BlockSpec(memory_space=pl.ANY),) * 2,
         scratch_shapes=[
-            pltpu.VMEM(turn.shape, jnp.float32),
+            pltpu.VMEM(s.shape, jnp.float32),
+            pltpu.VMEM((rows // k, k), jnp.float32),
+            pltpu.VMEM(s.shape, jnp.float32),
             pltpu.VMEM((k, k), jnp.float32),
             pltpu.SemaphoreType.DMA((chunks + 1,)),
+            pltpu.SemaphoreType.DMA((2,)),
         ],
         compiler_params=pltpu.CompilerParams(vmem_limit_bytes=VMEM_BYTES),
         name="modes",
-    )(table, turn)
+    )(table, s, last.reshape(rows // k, k))
 
 
 AXES = ("z", "y", "c", "x")
 NEAR = ("y", "c")
 FAR = ("z", "x")
+PIECE = 5
 
 
 def count(axes):
@@ -231,12 +252,6 @@
     return total
 
 
-def scatter_sum(table, axes):
-    n = count(axes)
-    blocks = table.reshape(n, table.shape[0] // n, table.shape[1])
-    return lax.all_to_all(blocks, axes, 0, 0, tiled=True).sum(axis=0)
-
-
 def exchange(block, axes):
     n = count(axes)
     copies = jnp.broadcast_to(block[None], (n, *block.shape))
@@ -244,16 +259,17 @@
 
 
 def total_moments(table):
-    block = scatter_sum(table, NEAR)
-    block = exchange(block, FAR).sum(axis=0)
-    return exchange(block, NEAR).reshape(table.shape)
+    n = count(NEAR)
+    pieces = table.reshape(n, table.shape[0] // n, 1, table.shape[1])
+    piece = lax.all_to_all(pieces, NEAR, 0, 0, tiled=True).sum(axis=0)
+    piece = exchange(piece, FAR).sum(axis=0)
+    return exchange(piece, NEAR).reshape(table.shape)
 
 
 def shards(snapshots, last_snapshot):
     row_count = snapshots.shape[0] * count(AXES)
-    table = moments(snapshots, last_snapshot)
-    turn = turn_columns(snapshots, last_snapshot)
-    return modes(row_count, total_moments(table), turn)
+    table = moments(snapshots, last_snapshot, PIECE * count(NEAR))
+    return modes(row_count, total_moments(table), snapshots, last_snapshot)
 
 
 def solution(mesh):

time: 72 us -> 69.5 us (0.965)
  blocking collectives: 49 us -> 58.9 us
  waiting for transfers between devices: 7.5 us -> 0 us
  starting transfers between devices: 5.55 us -> 0 us
  Pallas kernels: 8.2 us -> 9.39 us
    all_to_all x1 -> x2, blocking collectives: 27.4 us -> 37.6 us  [exchange(): return lax.all_to_all(copies, axes, 0, 0, tiled=True)]
    all_to_all x1 -> x0, waiting for transfers between devices: 7.5 us -> none  [exchange(): return lax.all_to_all(copies, axes, 0, 0, tiled=True)]
    all_to_all x1 -> x0, starting transfers between devices: 5.55 us -> none  [exchange(): return lax.all_to_all(copies, axes, 0, 0, tiled=True)]
    pallas_call x1, Pallas kernels: 5.65 us -> 7.21 us  [modes(): pl.pallas_call(functools.partial(modes_kernel, row_count, chunks), out_sh...]
    pallas_call x2 -> x1, Pallas kernels: 2.55 us -> 2.18 us  [moments(): pl.pallas_call(moments_kernel, out_shape=jax.ShapeDtypeStruct((table_rows...]
  transfers between devices with their start and end apart: 1 -> 0, of which waited for: 1 -> 0; matrix products, arithmetic and copies ran while one was open for 0% -> 0% of each run, Pallas kernels for 0% -> 0%
where the time goes in v4:
time: 69.5 us; the launch traced here: 69.2 us
  blocking collectives  58.9 us (85%)
  Pallas kernels  9.39 us (14%)
    all_to_all x2, blocking collectives, exchange(): return lax.all_to_all(copies, axes, 0, 0, tiled=True)  37.6 us
    all_to_all x1, blocking collectives, total_moments(): piece = lax.all_to_all(pieces, NEAR, 0, 0, tiled=True).sum(axis=0)  21.3 us
    pallas_call x1, Pallas kernels, modes(): pl.pallas_call(functools.partial(modes_kernel, row_count, chunks), out_sh...  7.21 us
    pallas_call x1, Pallas kernels, moments(): pl.pallas_call(moments_kernel, out_shape=jax.ShapeDtypeStruct((table_rows...  2.18 us

profile of v4, /device:TPU:1, one launch (start us, length us, event | category | flops | bytes accessed | tf_op | source)
XLA Modules:
  0.0 69.2 jit_solution(10841727871869171016)
XLA Ops:
  0.6 2.2 %moments.1 = f32[80,128]{1,0:T(8,128)} custom-call(f32[1024,128]{1,0:T(8,128)} %s_hbm.1, f32[8,128]{1,0:T(8,128)} %bitcast.5), custom_call_target="tpu_custom_call" | custom-call | tf_op jit(solution)/shard_map/moments/pallas_call | solution.py:73
  2.8 21.3 %all_to_all.15 = f32[16,5,1,128]{3,2,1,0:T(1,128)S(1)} all-to-all(f32[16,5,1,128]{3,2,1,0:T(1,128)} %bitcast.4), channel_id=1, replica_groups=mesh['z'=12,'y'=8,'c'=2,'x'=4] {'y','c'}, dimensions={0} | all-to-all | bytes 81920 | tf_op jit(solution)/shard_map/all_to_all | solution.py:264
  24.1 0.1 broadcast_in_dim.4
  24.2 24.5 %all_to_all.16 = f32[48,5,1,128]{3,2,1,0:T(1,128)S(1)} all-to-all(f32[48,5,1,128]{3,2,1,0:T(1,128)S(1)} %broadcast_in_dim.4), channel_id=1, replica_groups=mesh['z'=12,'y'=8,'c'=2,'x'=4] {'z','x'}, dimensions={0} | all-to-all | bytes 245760 | tf_op jit(solution)/shard_map/all_to_all | solution.py:258
  48.8 0.1 reduce_sum.19
  48.9 13.1 %all_to_all.17 = f32[16,5,1,128]{3,2,1,0:T(1,128)} all-to-all(f32[16,5,1,128]{3,2,1,0:T(1,128)S(1)} %broadcast_in_dim.5), channel_id=1, replica_groups=mesh['z'=12,'y'=8,'c'=2,'x'=4] {'y','c'}, dimensions={0} | all-to-all | bytes 81920 | tf_op jit(solution)/shard_map/all_to_all | solution.py:258
  62.0 7.2 %modes.1 = (f32[128,128]{1,0:T(8,128)}, f32[1024,128]{1,0:T(8,128)}) custom-call(f32[80,128]{1,0:T(8,128)} %bitcast.3, f32[1024,128]{1,0:T(8,128)} %s_hbm.1, f32[8,128]{1,0:T(8,128)} %bitcast.6), custom_call_target="tpu_custom_call" | custom-call | tf_op jit(solution)/shard_map/modes/pallas_call | solution.py:217
  (2 shorter events, 0.1 us)

commit v5 on v4

--- a/solution.py
+++ b/solution.py
@@ -240,9 +240,9 @@
 
 
 AXES = ("z", "y", "c", "x")
-NEAR = ("y", "c")
-FAR = ("z", "x")
-PIECE = 5
+NEAR = ("c", "x")
+FAR = ("y", "z")
+PIECE = 9
 
 
 def count(axes):
@@ -262,7 +262,8 @@
     n = count(NEAR)
     pieces = table.reshape(n, table.shape[0] // n, 1, table.shape[1])
     piece = lax.all_to_all(pieces, NEAR, 0, 0, tiled=True).sum(axis=0)
-    piece = exchange(piece, FAR).sum(axis=0)
+    for axis in FAR:
+        piece = exchange(piece, (axis,)).sum(axis=0)
     return exchange(piece, NEAR).reshape(table.shape)
 
 

time: 69.5 us -> 70.6 us (1.016)
  blocking collectives: 58.9 us -> 60 us
    all_to_all x2 -> x3, blocking collectives: 37.6 us -> 41.3 us  [exchange(): return lax.all_to_all(copies, axes, 0, 0, tiled=True)]
    all_to_all x1, blocking collectives: 21.3 us -> 18.7 us  [total_moments(): piece = lax.all_to_all(pieces, NEAR, 0, 0, tiled=True).sum(axis=0)]
where the time goes in v5:
time: 70.6 us; the launch traced here: 70.2 us
  blocking collectives  60 us (85%)
  Pallas kernels  9.36 us (13%)
    all_to_all x3, blocking collectives, exchange(): return lax.all_to_all(copies, axes, 0, 0, tiled=True)  41.3 us
    all_to_all x1, blocking collectives, total_moments(): piece = lax.all_to_all(pieces, NEAR, 0, 0, tiled=True).sum(axis=0)  18.7 us
    pallas_call x1, Pallas kernels, modes(): pl.pallas_call(functools.partial(modes_kernel, row_count, chunks), out_sh...  7.2 us
    pallas_call x1, Pallas kernels, moments(): pl.pallas_call(moments_kernel, out_shape=jax.ShapeDtypeStruct((table_rows...  2.16 us

profile of v5, /device:TPU:1, one launch (start us, length us, event | category | flops | bytes accessed | tf_op | source)
XLA Modules:
  0.0 70.2 jit_solution(13640768485475266174)
XLA Ops:
  0.6 2.2 %moments.1 = f32[72,128]{1,0:T(8,128)} custom-call(f32[1024,128]{1,0:T(8,128)} %s_hbm.1, f32[8,128]{1,0:T(8,128)} %bitcast.5), custom_call_target="tpu_custom_call" | custom-call | tf_op jit(solution)/shard_map/moments/pallas_call | solution.py:73
  2.8 18.7 %all_to_all.20 = f32[8,9,1,128]{3,2,1,0:T(1,128)S(1)} all-to-all(f32[8,9,1,128]{3,2,1,0:T(1,128)} %bitcast.4), channel_id=1, replica_groups=mesh['z'=12,'y'=8,'c'=2,'x'=4] {'c','x'}, dimensions={0} | all-to-all | bytes 73728 | tf_op jit(solution)/shard_map/all_to_all | solution.py:264
  21.5 9.3 %all_to_all.21 = f32[8,9,1,128]{3,2,1,0:T(1,128)S(1)} all-to-all(f32[8,9,1,128]{3,2,1,0:T(1,128)S(1)} %broadcast_in_dim.6), channel_id=1, replica_groups=mesh['z'=12,'y'=8,'c'=2,'x'=4] {'y'}, dimensions={0} | all-to-all | bytes 73728 | tf_op jit(solution)/shard_map/all_to_all | solution.py:258
  30.9 20.8 %all_to_all.22 = f32[12,9,1,128]{3,2,1,0:T(1,128)S(1)} all-to-all(f32[12,9,1,128]{3,2,1,0:T(1,128)S(1)} %broadcast_in_dim.7), channel_id=1, replica_groups=mesh['z'=12,'y'=8,'c'=2,'x'=4] {'z'}, dimensions={0} | all-to-all | bytes 110592 | tf_op jit(solution)/shard_map/all_to_all | solution.py:258
  51.8 11.1 %all_to_all.23 = f32[8,9,1,128]{3,2,1,0:T(1,128)} all-to-all(f32[8,9,1,128]{3,2,1,0:T(1,128)S(1)} %broadcast_in_dim.8), channel_id=1, replica_groups=mesh['z'=12,'y'=8,'c'=2,'x'=4] {'c','x'}, dimensions={0} | all-to-all | bytes 73728 | tf_op jit(solution)/shard_map/all_to_all | solution.py:258
  63.0 7.2 %modes.1 = (f32[128,128]{1,0:T(8,128)}, f32[1024,128]{1,0:T(8,128)}) custom-call(f32[72,128]{1,0:T(8,128)} %bitcast.3, f32[1024,128]{1,0:T(8,128)} %s_hbm.1, f32[8,128]{1,0:T(8,128)} %bitcast.6), custom_call_target="tpu_custom_call" | custom-call | tf_op jit(solution)/shard_map/modes/pallas_call | solution.py:217
  (6 shorter events, 0.2 us)

commit v6 on v4

--- a/solution.py
+++ b/solution.py
@@ -10,7 +10,7 @@
 
 HIGHEST = lax.Precision.HIGHEST
 B = 8
-VMEM_BYTES = 62000000
+VMEM_BYTES = 16 * 2**20
 TURN_AT = 8
 
 
@@ -160,15 +160,9 @@
     return jnp.concatenate([top, bottom], axis=0), flip[:, h : h + 1], table[h + 1 : h + 2, 0:1]
 
 
-def modes_kernel(row_count, chunks, table_ref, s_hbm, last_hbm, reduced_hbm, modes_hbm, *scratch):
-    turn_ref, last_ref, full_modes, small, sems, in_sems = scratch
+def modes_kernel(row_count, chunks, table_ref, s_ref, last_ref, reduced_hbm, modes_hbm, *scratch):
+    turn_ref, full_modes, small, sems = scratch
     k = table_ref.shape[1]
-    loads = [
-        pltpu.make_async_copy(last_hbm, last_ref, in_sems.at[0]),
-        pltpu.make_async_copy(s_hbm, turn_ref, in_sems.at[1]),
-    ]
-    for load in loads:
-        load.start()
     lane = lax.broadcasted_iota(jnp.int32, (k, k), 1)
     row = lax.broadcasted_iota(jnp.int32, (k, k), 0)
     full, last, square = unfold(table_ref[...])
@@ -178,15 +172,15 @@
     down = lax.rsqrt(jnp.sum(diagonal, axis=1, keepdims=True))
     unit = full * across * down
 
-    def turn_columns():
-        for load in loads:
-            load.wait()
-        columns = last_ref[...].T
-        for b in range(turn_ref.shape[0] // k):
-            part = slice(b * k, (b + 1) * k)
-            turn_ref[part, :] = jnp.where(lane == 0, columns[:, b : b + 1], turn_ref[part, :])
-
-    groups = inverse_rows([unit[n : n + B] for n in range(0, k, B)], k, {TURN_AT: turn_columns})
+    columns = last_ref[...].T
+
+    def turn_columns(b):
+        part = slice(b * k, (b + 1) * k)
+        turn_ref[part, :] = jnp.where(lane == 0, columns[:, b : b + 1], s_ref[part, :])
+
+    parts = turn_ref.shape[0] // k
+    between = {TURN_AT + b: functools.partial(turn_columns, b) for b in range(parts)}
+    groups = inverse_rows([unit[n : n + B] for n in range(0, k, B)], k, between)
     inv_t = jnp.where(row >= lane, jnp.concatenate(groups, axis=0), 0.0) * across
     turned_inv = pltpu.roll(inv_t, 1, 1)
     left = dot(inv_t, cross, ((1,), (0,)))
@@ -212,7 +206,7 @@
         copy.wait()
 
 
-def modes(row_count, table, s, last, chunks=4):
+def modes(row_count, table, s, last, chunks=2):
     rows, k = s.shape
     return pl.pallas_call(
         functools.partial(modes_kernel, row_count, chunks),
@@ -220,19 +214,13 @@
             jax.ShapeDtypeStruct((k, k), jnp.float32),
             jax.ShapeDtypeStruct(s.shape, jnp.float32),
         ),
-        in_specs=[
-            pl.BlockSpec(memory_space=pltpu.VMEM),
-            pl.BlockSpec(memory_space=pl.ANY),
-            pl.BlockSpec(memory_space=pl.ANY),
-        ],
+        in_specs=[pl.BlockSpec(memory_space=pltpu.VMEM)] * 3,
         out_specs=(pl.BlockSpec(memory_space=pl.ANY),) * 2,
         scratch_shapes=[
             pltpu.VMEM(s.shape, jnp.float32),
-            pltpu.VMEM((rows // k, k), jnp.float32),
             pltpu.VMEM(s.shape, jnp.float32),
             pltpu.VMEM((k, k), jnp.float32),
             pltpu.SemaphoreType.DMA((chunks + 1,)),
-            pltpu.SemaphoreType.DMA((2,)),
         ],
         compiler_params=pltpu.CompilerParams(vmem_limit_bytes=VMEM_BYTES),
         name="modes",

time: 69.5 us -> 67.5 us (0.971)
  Pallas kernels: 9.39 us -> 8.12 us
  blocking collectives: 58.9 us -> 58.2 us
    pallas_call x1, Pallas kernels: 7.21 us -> 5.89 us  [modes(): pl.pallas_call(functools.partial(modes_kernel, row_count, chunks), out_sh...]
where the time goes in v6:
time: 67.5 us; the launch traced here: 67.2 us
  blocking collectives  58.2 us (86%)
  Pallas kernels  8.12 us (12%)
    all_to_all x2, blocking collectives, exchange(): return lax.all_to_all(copies, axes, 0, 0, tiled=True)  36.9 us
    all_to_all x1, blocking collectives, total_moments(): piece = lax.all_to_all(pieces, NEAR, 0, 0, tiled=True).sum(axis=0)  21.3 us
    pallas_call x1, Pallas kernels, modes(): pl.pallas_call(functools.partial(modes_kernel, row_count, chunks), out_sh...  5.89 us
    pallas_call x1, Pallas kernels, moments(): pl.pallas_call(moments_kernel, out_shape=jax.ShapeDtypeStruct((table_rows...  2.22 us

profile of v6, /device:TPU:1, one launch (start us, length us, event | category | flops | bytes accessed | tf_op | source)
XLA Modules:
  0.0 67.2 jit_solution(2140269806432520349)
XLA Ops:
  0.6 0.0 copy-start
  0.6 2.2 %moments.1 = f32[80,128]{1,0:T(8,128)} custom-call(f32[1024,128]{1,0:T(8,128)} %s_ref.3, f32[8,128]{1,0:T(8,128)} %bitcast.4), custom_call_target="tpu_custom_call" | custom-call | tf_op jit(solution)/shard_map/moments/pallas_call | solution.py:73
  2.9 21.3 %all_to_all.15 = f32[16,5,1,128]{3,2,1,0:T(1,128)S(1)} all-to-all(f32[16,5,1,128]{3,2,1,0:T(1,128)} %bitcast.6), channel_id=1, replica_groups=mesh['z'=12,'y'=8,'c'=2,'x'=4] {'y','c'}, dimensions={0} | all-to-all | bytes 81920 | tf_op jit(solution)/shard_map/all_to_all | solution.py:252
  24.2 0.1 broadcast_in_dim.4
  24.3 24.5 %all_to_all.16 = f32[48,5,1,128]{3,2,1,0:T(1,128)S(1)} all-to-all(f32[48,5,1,128]{3,2,1,0:T(1,128)S(1)} %broadcast_in_dim.4), channel_id=1, replica_groups=mesh['z'=12,'y'=8,'c'=2,'x'=4] {'z','x'}, dimensions={0} | all-to-all | bytes 245760 | tf_op jit(solution)/shard_map/all_to_all | solution.py:246
  48.8 0.1 reduce_sum.19
  48.9 0.0 copy-start.1
  49.0 12.4 %all_to_all.17 = f32[16,5,1,128]{3,2,1,0:T(1,128)S(1)} all-to-all(f32[16,5,1,128]{3,2,1,0:T(1,128)S(1)} %broadcast_in_dim.5), channel_id=1, replica_groups=mesh['z'=12,'y'=8,'c'=2,'x'=4] {'y','c'}, dimensions={0} | all-to-all | bytes 81920 | tf_op jit(solution)/shard_map/all_to_all | solution.py:246
  61.3 0.0 copy-done
  61.3 0.0 copy-done.1
  61.3 5.9 %modes.1 = (f32[128,128]{1,0:T(8,128)}, f32[1024,128]{1,0:T(8,128)}) custom-call(f32[80,128]{1,0:T(8,128)S(1)} %bitcast.3, f32[1024,128]{1,0:T(8,128)S(1)} %copy-done, f32[8,128]{1,0:T(8,128)S(1)} %bitcast.5), custom_call_target="tpu_custom_call" | custom-call | tf_op jit(solution)/shard_map/modes/pallas_call | solution.py:211
  (2 shorter events, 0.1 us)
Async XLA Ops:
  0.6 60.7 %copy-start = (f32[1024,128]{1,0:T(8,128)S(1)}, f32[1024,128]{1,0:T(8,128)}, u32[]{:S(2)}) copy-start(f32[1024,128]{1,0:T(8,128)} %s_ref.3) | copy-start | bytes 1572868
  48.9 12.4 %copy-start.1 = (f32[1024]{0:T(1024)S(1)}, f32[1024]{0:T(1024)}, u32[]{:S(2)}) copy-start(f32[1024]{0:T(1024)} %param.3) | copy-start | bytes 12292

commit v7 on v6

--- a/solution.py
+++ b/solution.py
@@ -227,9 +227,9 @@
     )(table, s, last.reshape(rows // k, k))
 
 
-AXES = ("z", "y", "c", "x")
-NEAR = ("y", "c")
-FAR = ("z", "x")
+AXES = ("zh", "zl", "y", "c", "x")
+NEAR = ("zl", "c", "x")
+FAR = ("zh", "y")
 PIECE = 5
 
 
@@ -261,7 +261,7 @@
 
 
 def solution(mesh):
-    sizes = (12, 8, 2, 4)
+    sizes = (6, 2, 8, 2, 4)
     fine = Mesh(mesh.devices.reshape(sizes), AXES)
     in_specs = (P(AXES, None), P(AXES))
     out_specs = (P(), P(AXES, None))

time: 67.5 us -> 66.6 us (0.987)
  blocking collectives: 58.2 us -> 57.3 us
    all_to_all x1, blocking collectives: 21.3 us -> 19.6 us  [total_moments(): piece = lax.all_to_all(pieces, NEAR, 0, 0, tiled=True).sum(axis=0)]
    all_to_all x2, blocking collectives: 36.9 us -> 37.7 us  [exchange(): return lax.all_to_all(copies, axes, 0, 0, tiled=True)]
where the time goes in v7:
time: 66.6 us; the launch traced here: 66.4 us
  blocking collectives  57.3 us (86%)
  Pallas kernels  8.12 us (12%)
    all_to_all x2, blocking collectives, exchange(): return lax.all_to_all(copies, axes, 0, 0, tiled=True)  37.7 us
    all_to_all x1, blocking collectives, total_moments(): piece = lax.all_to_all(pieces, NEAR, 0, 0, tiled=True).sum(axis=0)  19.6 us
    pallas_call x1, Pallas kernels, modes(): pl.pallas_call(functools.partial(modes_kernel, row_count, chunks), out_sh...  5.89 us
    pallas_call x1, Pallas kernels, moments(): pl.pallas_call(moments_kernel, out_shape=jax.ShapeDtypeStruct((table_rows...  2.22 us

profile of v7, /device:TPU:1, one launch (start us, length us, event | category | flops | bytes accessed | tf_op | source)
XLA Modules:
  0.0 66.4 jit_solution(3560109338634761175)
XLA Ops:
  0.6 0.0 copy-start
  0.6 2.2 %moments.1 = f32[80,128]{1,0:T(8,128)} custom-call(f32[1024,128]{1,0:T(8,128)} %s_ref.3, f32[8,128]{1,0:T(8,128)} %bitcast.4), custom_call_target="tpu_custom_call" | custom-call | tf_op jit(solution)/shard_map/moments/pallas_call | solution.py:73
  2.9 19.6 %all_to_all.15 = f32[16,5,1,128]{3,2,1,0:T(1,128)S(1)} all-to-all(f32[16,5,1,128]{3,2,1,0:T(1,128)} %bitcast.6), channel_id=1, replica_groups=mesh['zh'=6,'zl'=2,'y'=8,'c'=2,'x'=4] {'zl','c','x'}, dimensions={0} | all-to-all | bytes 81920 | tf_op jit(solution)/shard_map/all_to_all | solution.py:252
  22.6 0.1 broadcast_in_dim.4
  22.6 27.3 %all_to_all.16 = f32[48,5,1,128]{3,2,1,0:T(1,128)S(1)} all-to-all(f32[48,5,1,128]{3,2,1,0:T(1,128)S(1)} %broadcast_in_dim.4), channel_id=1, replica_groups=mesh['zh'=6,'zl'=2,'y'=8,'c'=2,'x'=4] {'zh','y'}, dimensions={0} | all-to-all | bytes 245760 | tf_op jit(solution)/shard_map/all_to_all | solution.py:246
  50.0 0.1 reduce_sum.19
  50.1 0.0 copy-start.1
  50.1 10.3 %all_to_all.17 = f32[16,5,1,128]{3,2,1,0:T(1,128)S(1)} all-to-all(f32[16,5,1,128]{3,2,1,0:T(1,128)S(1)} %broadcast_in_dim.5), channel_id=1, replica_groups=mesh['zh'=6,'zl'=2,'y'=8,'c'=2,'x'=4] {'zl','c','x'}, dimensions={0} | all-to-all | bytes 81920 | tf_op jit(solution)/shard_map/all_to_all | solution.py:246
  60.5 0.0 copy-done
  60.5 0.0 copy-done.1
  60.5 5.9 %modes.1 = (f32[128,128]{1,0:T(8,128)}, f32[1024,128]{1,0:T(8,128)}) custom-call(f32[80,128]{1,0:T(8,128)S(1)} %bitcast.3, f32[1024,128]{1,0:T(8,128)S(1)} %copy-done, f32[8,128]{1,0:T(8,128)S(1)} %bitcast.5), custom_call_target="tpu_custom_call" | custom-call | tf_op jit(solution)/shard_map/modes/pallas_call | solution.py:211
  (2 shorter events, 0.1 us)
Async XLA Ops:
  0.6 59.8 %copy-start = (f32[1024,128]{1,0:T(8,128)S(1)}, f32[1024,128]{1,0:T(8,128)}, u32[]{:S(2)}) copy-start(f32[1024,128]{1,0:T(8,128)} %s_ref.3) | copy-start | bytes 1572868
  50.1 10.4 %copy-start.1 = (f32[1024]{0:T(1024)S(1)}, f32[1024]{0:T(1024)}, u32[]{:S(2)}) copy-start(f32[1024]{0:T(1024)} %param.3) | copy-start | bytes 12292

commit v8 on v7

--- a/solution.py
+++ b/solution.py
@@ -77,6 +77,25 @@
     )(s, last.reshape(rows // k, k))
 
 
+def far_update(groups_of_rows, q, g, groups):
+    b, k = q[0].shape
+    sub = lax.broadcasted_iota(jnp.int32, (b, k), 0)
+    mine = q[0]
+    for j in range(1, b):
+        mine = jnp.where(sub == j, q[j], mine)
+    zero = jnp.zeros((b, k), jnp.float32)
+    high, middle, low = split(jnp.concatenate([zero] * g + [mine] + [zero] * (groups - 1 - g), axis=0))
+    left_high, left_middle, left_low = split(jnp.concatenate(groups_of_rows, axis=0))
+    wide = jnp.concatenate([high, middle], axis=1)
+    main = product(
+        jnp.concatenate([left_high, left_middle], axis=1), jnp.concatenate([wide, wide], axis=0)
+    )
+    small = product(
+        jnp.concatenate([left_high, left_low], axis=1), jnp.concatenate([low, high], axis=0)
+    )
+    return (small + main[:, k:]) + main[:, :k]
+
+
 def inverse_rows(w, k, between):
     lane = lax.broadcasted_iota(jnp.int32, (B, k), 1)
     sub = lax.broadcasted_iota(jnp.int32, (B, k), 0)
@@ -91,7 +110,8 @@
             between[g]()
         at = g * B
         inside = (lane >= at) & (lane < at + B)
-        columns = [wide(w[g][:, at + j : at + j + 1]) for j in range(B)]
+        if not g:
+            columns = [wide(w[0][:, j : j + 1]) for j in range(B)]
         e = {(i, j): wide(columns[j][i : i + 1, :]) for j in range(B) for i in range(j + 1)}
         p = [
             jnp.where(inside, (lane == at + i).astype(jnp.float32), wide(w[g][i : i + 1, :]))
@@ -101,6 +121,7 @@
         if inner:
             s = [wide(w[g + 1][:, at + j : at + j + 1]) for j in range(B)]
             after = jnp.where(inside, 0.0, w[g + 1])
+            columns = [wide(w[g + 1][:, at + B + j : at + B + j + 1]) for j in range(B)]
         low, inv, pivot = {}, [None] * B, [None] * B
         for j in range(0, B, 2):
             n = j + 1
@@ -124,6 +145,10 @@
                 for m in range(j + 2, B):
                     s[m] = (s[m] - s[j] * low[m, j]) - s[n] * low[m, n]
                 after = after - (s[j] * (p[j] * ra) + s[n] * (p[n] * rs))
+                sj, sn = s[j] * ra, s[n] * rs
+                for m in range(B):
+                    both = sj * wide(s[j][m : m + 1, :]) + sn * wide(s[n][m : m + 1, :])
+                    columns[m] = columns[m] - both
         rows = None
         for j in range(B):
             y = p[j] * lax.rsqrt(pivot[j])
@@ -138,11 +163,16 @@
         for j in range(B - 1, 0, -1):
             for i in range(j):
                 q[i] = q[i] - low[j, i] * q[j]
-        for h in range(g + 2, groups):
+        direct = min(g + 3, groups) if groups - (g + 3) >= 2 else groups
+        for h in range(g + 2, direct):
             t = [wide(w[h][:, at + j : at + j + 1]) * q[j] for j in range(B)]
             while len(t) > 1:
                 t = [t[n] + t[n + 1] for n in range(0, len(t), 2)]
             w[h] = jnp.where(inside, 0.0, w[h]) - t[0]
+        if direct < groups:
+            rest = far_update(w[direct:], q, g, groups)
+            for n, h in enumerate(range(direct, groups)):
+                w[h] = jnp.where(inside, 0.0, w[h]) - rest[n * B : (n + 1) * B]
     return out
 
 
@@ -228,7 +258,7 @@
 
 
 AXES = ("zh", "zl", "y", "c", "x")
-NEAR = ("zl", "c", "x")
+NEAR = ("c", "zl", "x")
 FAR = ("zh", "y")
 PIECE = 5
 

time: 66.6 us -> 65.4 us (0.982)
  Pallas kernels: 8.12 us -> 6.72 us
    pallas_call x1, Pallas kernels: 5.89 us -> 4.49 us  [modes(): pl.pallas_call(functools.partial(modes_kernel, row_count, chunks), out_sh...]
where the time goes in v8:
time: 65.4 us; the launch traced here: 65.1 us
  blocking collectives  57.5 us (88%)
  Pallas kernels  6.72 us (10%)
  between operations  0.66 us (1%)
    all_to_all x2, blocking collectives, exchange(): return lax.all_to_all(copies, axes, 0, 0, tiled=True)  37.8 us
    all_to_all x1, blocking collectives, total_moments(): piece = lax.all_to_all(pieces, NEAR, 0, 0, tiled=True).sum(axis=0)  19.6 us
    pallas_call x1, Pallas kernels, modes(): pl.pallas_call(functools.partial(modes_kernel, row_count, chunks), out_sh...  4.49 us
    pallas_call x1, Pallas kernels, moments(): pl.pallas_call(moments_kernel, out_shape=jax.ShapeDtypeStruct((table_rows...  2.22 us

profile of v8, /device:TPU:1, one launch (start us, length us, event | category | flops | bytes accessed | tf_op | source)
XLA Modules:
  0.0 65.1 jit_solution(8208787787627613839)
XLA Ops:
  0.6 0.0 copy-start
  0.6 2.2 %moments.1 = f32[80,128]{1,0:T(8,128)} custom-call(f32[1024,128]{1,0:T(8,128)} %s_ref.3, f32[8,128]{1,0:T(8,128)} %bitcast.4), custom_call_target="tpu_custom_call" | custom-call | tf_op jit(solution)/shard_map/moments/pallas_call | solution.py:73
  2.9 19.6 %all_to_all.15 = f32[16,5,1,128]{3,2,1,0:T(1,128)S(1)} all-to-all(f32[16,5,1,128]{3,2,1,0:T(1,128)} %bitcast.6), channel_id=1, replica_groups=mesh['zh'=6,'zl'=2,'y'=8,'c'=2,'x'=4] {'c','zl','x'}, dimensions={0} | all-to-all | bytes 81920 | tf_op jit(solution)/shard_map/all_to_all | solution.py:282
  22.6 0.1 broadcast_in_dim.4
  22.6 27.4 %all_to_all.16 = f32[48,5,1,128]{3,2,1,0:T(1,128)S(1)} all-to-all(f32[48,5,1,128]{3,2,1,0:T(1,128)S(1)} %broadcast_in_dim.4), channel_id=1, replica_groups=mesh['zh'=6,'zl'=2,'y'=8,'c'=2,'x'=4] {'zh','y'}, dimensions={0} | all-to-all | bytes 245760 | tf_op jit(solution)/shard_map/all_to_all | solution.py:276
  50.1 0.1 reduce_sum.19
  50.2 0.0 copy-start.1
  50.2 10.4 %all_to_all.17 = f32[16,5,1,128]{3,2,1,0:T(1,128)S(1)} all-to-all(f32[16,5,1,128]{3,2,1,0:T(1,128)S(1)} %broadcast_in_dim.5), channel_id=1, replica_groups=mesh['zh'=6,'zl'=2,'y'=8,'c'=2,'x'=4] {'c','zl','x'}, dimensions={0} | all-to-all | bytes 81920 | tf_op jit(solution)/shard_map/all_to_all | solution.py:276
  60.6 0.0 copy-done
  60.6 0.0 copy-done.1
  60.6 4.5 %modes.1 = (f32[128,128]{1,0:T(8,128)}, f32[1024,128]{1,0:T(8,128)}) custom-call(f32[80,128]{1,0:T(8,128)S(1)} %bitcast.3, f32[1024,128]{1,0:T(8,128)S(1)} %copy-done, f32[8,128]{1,0:T(8,128)S(1)} %bitcast.5), custom_call_target="tpu_custom_call" | custom-call | tf_op jit(solution)/shard_map/modes/pallas_call | solution.py:241
  (2 shorter events, 0.1 us)
Async XLA Ops:
  0.6 60.0 %copy-start = (f32[1024,128]{1,0:T(8,128)S(1)}, f32[1024,128]{1,0:T(8,128)}, u32[]{:S(2)}) copy-start(f32[1024,128]{1,0:T(8,128)} %s_ref.3) | copy-start | bytes 1572868
  50.2 10.4 %copy-start.1 = (f32[1024]{0:T(1024)S(1)}, f32[1024]{0:T(1024)}, u32[]{:S(2)}) copy-start(f32[1024]{0:T(1024)} %param.3) | copy-start | bytes 12292

commit v9 on v8

--- a/solution.py
+++ b/solution.py
@@ -8,16 +8,9 @@
 from jax.sharding import Mesh
 from jax.sharding import PartitionSpec as P
 
-HIGHEST = lax.Precision.HIGHEST
 B = 8
 VMEM_BYTES = 16 * 2**20
 TURN_AT = 8
-
-
-def dot(left, right, dims):
-    return lax.dot_general(
-        left, right, (dims, ((), ())), precision=HIGHEST, preferred_element_type=jnp.float32
-    )
 
 
 def split(x):
@@ -190,13 +183,32 @@
     return jnp.concatenate([top, bottom], axis=0), flip[:, h : h + 1], table[h + 1 : h + 2, 0:1]
 
 
+def stack(x):
+    high, middle, low = split(x)
+    return jnp.concatenate([high, middle], axis=1), jnp.concatenate([high, low], axis=1)
+
+
+def stacked_product(lead, rest, right):
+    high, middle, low = right
+    k = high.shape[0]
+    dims = (((1,), (1,)), ((), ()))
+    twice = [jnp.concatenate([part, part], axis=1) for part in (high, middle)]
+    main = lax.dot_general(
+        lead, jnp.concatenate(twice, axis=0), dims, preferred_element_type=jnp.float32
+    )
+    small = lax.dot_general(
+        rest, jnp.concatenate([low, high], axis=1), dims, preferred_element_type=jnp.float32
+    )
+    return (small + main[:, k:]) + main[:, :k]
+
+
 def modes_kernel(row_count, chunks, table_ref, s_ref, last_ref, reduced_hbm, modes_hbm, *scratch):
-    turn_ref, full_modes, small, sems = scratch
+    lead_ref, rest_ref, full_modes, small, sems = scratch
     k = table_ref.shape[1]
     lane = lax.broadcasted_iota(jnp.int32, (k, k), 1)
     row = lax.broadcasted_iota(jnp.int32, (k, k), 0)
     full, last, square = unfold(table_ref[...])
-    cross = jnp.where(lane == 0, last, full)
+    crossed = split(jnp.where(lane == 0, last, full).T)
     diagonal = jnp.where(row == lane, full, 0.0)
     across = lax.rsqrt(jnp.sum(diagonal, axis=0, keepdims=True))
     down = lax.rsqrt(jnp.sum(diagonal, axis=1, keepdims=True))
@@ -206,16 +218,19 @@
 
     def turn_columns(b):
         part = slice(b * k, (b + 1) * k)
-        turn_ref[part, :] = jnp.where(lane == 0, columns[:, b : b + 1], s_ref[part, :])
-
-    parts = turn_ref.shape[0] // k
+        lead_ref[part, :], rest_ref[part, :] = stack(
+            jnp.where(lane == 0, columns[:, b : b + 1], s_ref[part, :])
+        )
+
+    parts = s_ref.shape[0] // k
     between = {TURN_AT + b: functools.partial(turn_columns, b) for b in range(parts)}
     groups = inverse_rows([unit[n : n + B] for n in range(0, k, B)], k, between)
     inv_t = jnp.where(row >= lane, jnp.concatenate(groups, axis=0), 0.0) * across
     turned_inv = pltpu.roll(inv_t, 1, 1)
-    left = dot(inv_t, cross, ((1,), (0,)))
-    full_modes[...] = dot(turn_ref[...], turned_inv, ((1,), (1,)))
-    reduced = dot(left, turned_inv, ((1,), (1,)))
+    left = stacked_product(*stack(inv_t), crossed)
+    turned_parts = split(turned_inv)
+    full_modes[...] = stacked_product(lead_ref[...], rest_ref[...], turned_parts)
+    reduced = stacked_product(*stack(left), turned_parts)
     small[...] = reduced
     copies = [pltpu.make_async_copy(small, reduced_hbm, sems.at[chunks])]
     copies[0].start()
@@ -247,7 +262,8 @@
         in_specs=[pl.BlockSpec(memory_space=pltpu.VMEM)] * 3,
         out_specs=(pl.BlockSpec(memory_space=pl.ANY),) * 2,
         scratch_shapes=[
-            pltpu.VMEM(s.shape, jnp.float32),
+            pltpu.VMEM((rows, 2 * k), jnp.bfloat16),
+            pltpu.VMEM((rows, 2 * k), jnp.bfloat16),
             pltpu.VMEM(s.shape, jnp.float32),
             pltpu.VMEM((k, k), jnp.float32),
             pltpu.SemaphoreType.DMA((chunks + 1,)),
@@ -259,7 +275,7 @@
 
 AXES = ("zh", "zl", "y", "c", "x")
 NEAR = ("c", "zl", "x")
-FAR = ("zh", "y")
+FAR = ("y", "zh")
 PIECE = 5
 
 

time: 65.4 us -> 65.2 us (level)
  no operation moved by 1% of the time
where the time goes in v9:
time: 65.2 us; the launch traced here: 64.9 us
  blocking collectives  57.4 us (88%)
  Pallas kernels  6.59 us (10%)
  between operations  0.66 us (1%)
    all_to_all x2, blocking collectives, exchange(): return lax.all_to_all(copies, axes, 0, 0, tiled=True)  37.7 us
    all_to_all x1, blocking collectives, total_moments(): piece = lax.all_to_all(pieces, NEAR, 0, 0, tiled=True).sum(axis=0)  19.6 us
    pallas_call x1, Pallas kernels, modes(): pl.pallas_call(functools.partial(modes_kernel, row_count, chunks), out_sh...  4.36 us
    pallas_call x1, Pallas kernels, moments(): pl.pallas_call(moments_kernel, out_shape=jax.ShapeDtypeStruct((table_rows...  2.22 us

profile of v9, /device:TPU:1, one launch (start us, length us, event | category | flops | bytes accessed | tf_op | source)
XLA Modules:
  0.0 64.9 jit_solution(17946922227473228309)
XLA Ops:
  0.6 0.0 copy-start
  0.6 2.2 %moments.1 = f32[80,128]{1,0:T(8,128)} custom-call(f32[1024,128]{1,0:T(8,128)} %s_ref.3, f32[8,128]{1,0:T(8,128)} %bitcast.4), custom_call_target="tpu_custom_call" | custom-call | tf_op jit(solution)/shard_map/moments/pallas_call | solution.py:66
  2.9 19.6 %all_to_all.15 = f32[16,5,1,128]{3,2,1,0:T(1,128)S(1)} all-to-all(f32[16,5,1,128]{3,2,1,0:T(1,128)} %bitcast.6), channel_id=1, replica_groups=mesh['zh'=6,'zl'=2,'y'=8,'c'=2,'x'=4] {'c','zl','x'}, dimensions={0} | all-to-all | bytes 81920 | tf_op jit(solution)/shard_map/all_to_all | solution.py:298
  22.6 0.1 broadcast_in_dim.4
  22.6 27.2 %all_to_all.16 = f32[48,5,1,128]{3,2,1,0:T(1,128)S(1)} all-to-all(f32[48,5,1,128]{3,2,1,0:T(1,128)S(1)} %broadcast_in_dim.4), channel_id=1, replica_groups=mesh['zh'=6,'zl'=2,'y'=8,'c'=2,'x'=4] {'y','zh'}, dimensions={0} | all-to-all | bytes 245760 | tf_op jit(solution)/shard_map/all_to_all | solution.py:292
  49.8 0.1 reduce_sum.19
  50.0 0.0 copy-start.1
  50.0 10.5 %all_to_all.17 = f32[16,5,1,128]{3,2,1,0:T(1,128)S(1)} all-to-all(f32[16,5,1,128]{3,2,1,0:T(1,128)S(1)} %broadcast_in_dim.5), channel_id=1, replica_groups=mesh['zh'=6,'zl'=2,'y'=8,'c'=2,'x'=4] {'c','zl','x'}, dimensions={0} | all-to-all | bytes 81920 | tf_op jit(solution)/shard_map/all_to_all | solution.py:292
  60.5 0.0 copy-done
  60.5 0.0 copy-done.1
  60.5 4.4 %modes.1 = (f32[128,128]{1,0:T(8,128)}, f32[1024,128]{1,0:T(8,128)}) custom-call(f32[80,128]{1,0:T(8,128)S(1)} %bitcast.3, f32[1024,128]{1,0:T(8,128)S(1)} %copy-done, f32[8,128]{1,0:T(8,128)S(1)} %bitcast.5), custom_call_target="tpu_custom_call" | custom-call | tf_op jit(solution)/shard_map/modes/pallas_call | solution.py:256
  (2 shorter events, 0.1 us)
Async XLA Ops:
  0.6 59.9 %copy-start = (f32[1024,128]{1,0:T(8,128)S(1)}, f32[1024,128]{1,0:T(8,128)}, u32[]{:S(2)}) copy-start(f32[1024,128]{1,0:T(8,128)} %s_ref.3) | copy-start | bytes 1572868
  50.0 10.6 %copy-start.1 = (f32[1024]{0:T(1024)S(1)}, f32[1024]{0:T(1024)}, u32[]{:S(2)}) copy-start(f32[1024]{0:T(1024)} %param.3) | copy-start | bytes 12292

commit v10 on v9

--- a/solution.py
+++ b/solution.py
@@ -112,9 +112,14 @@
         ]
         inner = g < groups - 1
         if inner:
-            s = [wide(w[g + 1][:, at + j : at + j + 1]) for j in range(B)]
+            s = ahead if g else [wide(w[1][:, j : j + 1]) for j in range(B)]
             after = jnp.where(inside, 0.0, w[g + 1])
             columns = [wide(w[g + 1][:, at + B + j : at + B + j + 1]) for j in range(B)]
+        second = g + 2 < groups
+        if second:
+            s2 = [wide(w[g + 2][:, at + j : at + j + 1]) for j in range(B)]
+            ahead = [wide(w[g + 2][:, at + B + j : at + B + j + 1]) for j in range(B)]
+            after2 = jnp.where(inside, 0.0, w[g + 2])
         low, inv, pivot = {}, [None] * B, [None] * B
         for j in range(0, B, 2):
             n = j + 1
@@ -138,10 +143,19 @@
                 for m in range(j + 2, B):
                     s[m] = (s[m] - s[j] * low[m, j]) - s[n] * low[m, n]
                 after = after - (s[j] * (p[j] * ra) + s[n] * (p[n] * rs))
+                pj, pn = p[j] * ra, p[n] * rs
                 sj, sn = s[j] * ra, s[n] * rs
+                if second:
+                    s2[n] = s2[n] - s2[j] * low[n, j]
+                    for m in range(j + 2, B):
+                        s2[m] = (s2[m] - s2[j] * low[m, j]) - s2[n] * low[m, n]
+                    after2 = after2 - (s2[j] * pj + s2[n] * pn)
+                    tj, tn = s2[j] * ra, s2[n] * rs
                 for m in range(B):
-                    both = sj * wide(s[j][m : m + 1, :]) + sn * wide(s[n][m : m + 1, :])
-                    columns[m] = columns[m] - both
+                    first, other = wide(s[j][m : m + 1, :]), wide(s[n][m : m + 1, :])
+                    columns[m] = columns[m] - (sj * first + sn * other)
+                    if second:
+                        ahead[m] = ahead[m] - (tj * first + tn * other)
         rows = None
         for j in range(B):
             y = p[j] * lax.rsqrt(pivot[j])
@@ -156,12 +170,8 @@
         for j in range(B - 1, 0, -1):
             for i in range(j):
                 q[i] = q[i] - low[j, i] * q[j]
-        direct = min(g + 3, groups) if groups - (g + 3) >= 2 else groups
-        for h in range(g + 2, direct):
-            t = [wide(w[h][:, at + j : at + j + 1]) * q[j] for j in range(B)]
-            while len(t) > 1:
-                t = [t[n] + t[n + 1] for n in range(0, len(t), 2)]
-            w[h] = jnp.where(inside, 0.0, w[h]) - t[0]
+        w[g + 2] = after2
+        direct = g + 3
         if direct < groups:
             rest = far_update(w[direct:], q, g, groups)
             for n, h in enumerate(range(direct, groups)):
@@ -251,7 +261,7 @@
         copy.wait()
 
 
-def modes(row_count, table, s, last, chunks=2):
+def modes(row_count, table, s, last, chunks=4):
     rows, k = s.shape
     return pl.pallas_call(
         functools.partial(modes_kernel, row_count, chunks),

time: 65.2 us -> 65.2 us (level)
  no operation moved by 1% of the time
where the time goes in v10:
time: 65.2 us; the launch traced here: 64.9 us
  blocking collectives  57.4 us (88%)
  Pallas kernels  6.59 us (10%)
  between operations  0.66 us (1%)
    all_to_all x2, blocking collectives, exchange(): return lax.all_to_all(copies, axes, 0, 0, tiled=True)  37.7 us
    all_to_all x1, blocking collectives, total_moments(): piece = lax.all_to_all(pieces, NEAR, 0, 0, tiled=True).sum(axis=0)  19.6 us
    pallas_call x1, Pallas kernels, modes(): pl.pallas_call(functools.partial(modes_kernel, row_count, chunks), out_sh...  4.37 us
    pallas_call x1, Pallas kernels, moments(): pl.pallas_call(moments_kernel, out_shape=jax.ShapeDtypeStruct((table_rows...  2.22 us

profile of v10, /device:TPU:1, one launch (start us, length us, event | category | flops | bytes accessed | tf_op | source)
XLA Modules:
  0.0 64.9 jit_solution(10503570009823793531)
XLA Ops:
  0.6 0.0 copy-start
  0.6 2.2 %moments.1 = f32[80,128]{1,0:T(8,128)} custom-call(f32[1024,128]{1,0:T(8,128)} %s_ref.3, f32[8,128]{1,0:T(8,128)} %bitcast.4), custom_call_target="tpu_custom_call" | custom-call | tf_op jit(solution)/shard_map/moments/pallas_call | solution.py:66
  2.9 19.6 %all_to_all.15 = f32[16,5,1,128]{3,2,1,0:T(1,128)S(1)} all-to-all(f32[16,5,1,128]{3,2,1,0:T(1,128)} %bitcast.6), channel_id=1, replica_groups=mesh['zh'=6,'zl'=2,'y'=8,'c'=2,'x'=4] {'c','zl','x'}, dimensions={0} | all-to-all | bytes 81920 | tf_op jit(solution)/shard_map/all_to_all | solution.py:308
  22.6 0.1 broadcast_in_dim.4
  22.6 27.2 %all_to_all.16 = f32[48,5,1,128]{3,2,1,0:T(1,128)S(1)} all-to-all(f32[48,5,1,128]{3,2,1,0:T(1,128)S(1)} %broadcast_in_dim.4), channel_id=1, replica_groups=mesh['zh'=6,'zl'=2,'y'=8,'c'=2,'x'=4] {'y','zh'}, dimensions={0} | all-to-all | bytes 245760 | tf_op jit(solution)/shard_map/all_to_all | solution.py:302
  49.8 0.1 reduce_sum.19
  50.0 0.0 copy-start.1
  50.0 10.5 %all_to_all.17 = f32[16,5,1,128]{3,2,1,0:T(1,128)S(1)} all-to-all(f32[16,5,1,128]{3,2,1,0:T(1,128)S(1)} %broadcast_in_dim.5), channel_id=1, replica_groups=mesh['zh'=6,'zl'=2,'y'=8,'c'=2,'x'=4] {'c','zl','x'}, dimensions={0} | all-to-all | bytes 81920 | tf_op jit(solution)/shard_map/all_to_all | solution.py:302
  60.5 0.0 copy-done
  60.5 0.0 copy-done.1
  60.5 4.4 %modes.1 = (f32[128,128]{1,0:T(8,128)}, f32[1024,128]{1,0:T(8,128)}) custom-call(f32[80,128]{1,0:T(8,128)S(1)} %bitcast.3, f32[1024,128]{1,0:T(8,128)S(1)} %copy-done, f32[8,128]{1,0:T(8,128)S(1)} %bitcast.5), custom_call_target="tpu_custom_call" | custom-call | tf_op jit(solution)/shard_map/modes/pallas_call | solution.py:266
  (2 shorter events, 0.1 us)
Async XLA Ops:
  0.6 59.9 %copy-start = (f32[1024,128]{1,0:T(8,128)S(1)}, f32[1024,128]{1,0:T(8,128)}, u32[]{:S(2)}) copy-start(f32[1024,128]{1,0:T(8,128)} %s_ref.3) | copy-start | bytes 1572868
  50.0 10.6 %copy-start.1 = (f32[1024]{0:T(1024)S(1)}, f32[1024]{0:T(1024)}, u32[]{:S(2)}) copy-start(f32[1024]{0:T(1024)} %param.3) | copy-start | bytes 12292
